TPU v7x, 32 devices: a whole 2x2x4 slice. The times are simulated.
32 devices in a mesh: clip: 2 (over core), span: 4 (over y, x), band: 4 (over z).
Axes of the slice: x: 2, y: 2, z: 4, core: 2. Of those that a mesh axis runs over, the one named last changes fastest.
Arguments:
- frames: bfloat16 [32, 48, 768], P(('clip', 'span'), 'band'), may hold values from -6 to 6
- segments: int32 [8], replicated, may hold values from 0 to 3, never falling along the last dimension, each value on 1 to 4 neighbouring positions
- targets: float32 [4], replicated, may hold values from -4 to 4
- in_weight: bfloat16 [3, 3, 9, 96], replicated, may hold values from -0.625 to 0.625
- in_bias: float32 [96], replicated, may hold values from -2 to 2
- gain_one: float32 [96], replicated, may hold values from 0.1 to 1.9
- mid_weight: bfloat16 [3, 3, 288, 96], replicated, may hold values from -0.125 to 0.125
- mid_bias: float32 [96], replicated, may hold values from -2 to 2
- gain_two: float32 [96], replicated, may hold values from 0.1 to 1.9
- out_weight: bfloat16 [3, 3, 288, 96], replicated, may hold values from -0.125 to 0.125
- out_bias: float32 [96], replicated, may hold values from -2 to 2
- head_weight: float32 [96], replicated, may hold values from -0.625 to 0.625
- head_bias: float32 [1], replicated, may hold values from -3 to 3
Outputs:
- features: bfloat16 [32, 48, 24576], P(('clip', 'span'), 'band')
- scores: float32 [4], replicated
- loss: float32 [], replicated
Inputs may be any that keep to these rules, and one draw needn't show every extreme that they name: `segments`: clip numbers never fall along the spans; every clip has 1 to 4 spans and one has exactly 4.
All inputs are finite; a program needn't handle non-finite values.
Results may differ from a plain program's by a relative error of at most 0.008.
Values may be sent and summed in bfloat16 or wider, within the bound.
No kernel may reach another device: no remote copies, remote signals or barrier semaphores. Data moves between devices by JAX's collectives and lax.ppermute only.
A program may use at most 192 MiB of HBM per device.

v0:
```python
import functools

import jax
import jax.numpy as jnp
from jax import lax
from jax.experimental import pallas as pl
from jax.experimental.pallas import tpu as pltpu
from jax.sharding import PartitionSpec as P

BF16 = jnp.bfloat16
F32 = jnp.float32
POSITION = ("clip", "span")
SLOT = 32


def moved(block, axis, distance):
    count = lax.axis_size(axis)
    route = [(i, i + distance) for i in range(count) if 0 <= i + distance < count]
    return lax.ppermute(block, axis, route)


def total_over(value, axis):
    count = lax.axis_size(axis)
    if count & (count - 1):
        return lax.psum(value, axis)
    step = 1
    while step < count:
        value = value + lax.ppermute(value, axis, [(i, i ^ step) for i in range(count)])
        step *= 2
    return value


def shifted_sum(product, channels, first, last):
    width = product.shape[1]
    left = jnp.where(first, 0.0, pltpu.roll(product[:channels], 1, 1))
    right = jnp.where(last, 0.0, pltpu.roll(product[2 * channels :], width - 1, 1))
    return product[channels : 2 * channels] + left + right


def rms_silu(value, gain):
    scale = lax.rsqrt(jnp.mean(value * value, axis=0, keepdims=True) + 1e-06)
    half = value * scale * (0.5 * gain)
    return half + half * jnp.tanh(half)


def block_kernel(
    flags, x_ref, win_ref, wmid_ref, wout_ref, cols_ref, out_ref, sum_ref,
    act_one, act_two, h0_ref, table, total, stage,
):
    rows, count = out_ref.shape[0], out_ref.shape[1]
    channels = win_ref.shape[0]
    width = x_ref.shape[3]
    keep, top, bottom = flags[0], flags[1], flags[2]

    columns = jnp.transpose(cols_ref[...])
    for j in range(6):
        table[j] = jnp.broadcast_to(columns[:, j : j + 1], (channels, width))
    total[...] = jnp.zeros_like(total)
    pixel = lax.broadcasted_iota(jnp.int32, (channels, width), 1)
    first, last = pixel == 0, pixel == width - 1

    def row_mask(row, rim, extent):
        inside = jnp.where(row < rim, top, 1.0)
        return inside * jnp.where(row >= extent - rim, bottom, 1.0)

    def first_row(row, carry):
        mask = row_mask(row, 2, rows + 4)
        for t in range(count + 4):
            taps = x_ref[t : t + 3, row].reshape(3 * SLOT, width)
            h0 = jnp.dot(win_ref[...], taps, preferred_element_type=F32) + table[0]
            h0 = h0.astype(BF16)
            if t >= 4:
                h0_ref[row, t - 4] = h0
            act = rms_silu(h0.astype(F32), table[1]) * (mask * keep if t < 4 else mask)
            act_one[row, t] = act.astype(BF16)
        return carry

    lax.fori_loop(0, rows + 4, first_row, 0)

    def taps_of(source, row, t):
        return jnp.concatenate(
            [source[row + dr, t : t + 3].reshape(3 * channels, width) for dr in range(3)], axis=0
        )

    def middle_row(row, carry):
        mask = row_mask(row, 1, rows + 2)
        for t in range(count + 2):
            product = jnp.dot(wmid_ref[...], taps_of(act_one, row, t), preferred_element_type=F32)
            h1 = shifted_sum(product, channels, first, last) + table[2]
            act = rms_silu(h1, table[3]) * (mask * keep if t < 2 else mask)
            act_two[row, t] = act.astype(BF16)
        return carry

    lax.fori_loop(0, rows + 2, middle_row, 0)

    lane = lax.broadcasted_iota(jnp.int32, (width // 4, count, 128), 2)

    def last_row(row, carry):
        for t in range(count):
            product = jnp.dot(wout_ref[...], taps_of(act_two, row, t), preferred_element_type=F32)
            value = shifted_sum(product, channels, first, last) + table[4]
            value = (value + h0_ref[row + 2, t].astype(F32)).astype(BF16).astype(F32)
            total[...] += value
            padded = jnp.concatenate([value, jnp.zeros((128 - channels, width), F32)], axis=0)
            stage[:, t, :] = jnp.transpose(padded)
        pixels = stage[...].reshape(width // 4, 4, count, 128)
        one = pltpu.roll(pixels[:, 1], 96, 2)
        two = pltpu.roll(pixels[:, 2], 64, 2)
        three = pltpu.roll(pixels[:, 3], 32, 2)
        tiles = [
            jnp.where(lane < 96, pixels[:, 0], one).astype(BF16),
            jnp.where(lane < 64, one, two).astype(BF16),
            jnp.where(lane < 32, two, three).astype(BF16),
        ]
        for group in range(width // 4):
            for j in range(3):
                at = (3 * group + j) * 128
                out_ref[row, :, at : at + 128] = tiles[j][group]
        return carry

    lax.fori_loop(0, rows, last_row, 0)
    sum_ref[...] = jnp.broadcast_to(jnp.sum(total[...] * table[5], keepdims=True), sum_ref.shape)


def local(
    frames, segments, targets, in_weight, in_bias, gain_one, mid_weight, mid_bias,
    gain_two, out_weight, out_bias, head_weight, head_bias,
):
    count, rows = frames.shape[0], frames.shape[1]
    channels = in_bias.shape[0]
    width = frames.shape[2] // 3
    position = lax.axis_index(POSITION)
    band = lax.axis_index("band")
    clip_id = segments[position]
    before = segments[jnp.maximum(position - 1, 0)]
    keep = ((position > 0) & (clip_id == before)).astype(F32)
    older = segments[jnp.maximum(position - 2, 0)]
    keep_older = ((position > 1) & (older == before)).astype(F32) * keep
    flags = jnp.stack(
        [keep, (band > 0).astype(F32), (band < lax.axis_size("band") - 1).astype(F32)]
    )

    colours = frames.reshape(count, rows, width, 3).transpose(0, 1, 3, 2)
    low = moved(colours[:, rows - 3 :], "band", 1)
    high = moved(colours[:, :3], "band", -1)
    wide = jnp.concatenate([low, colours, high], axis=1)
    previous = moved(wide, POSITION, 1) * keep.astype(BF16)
    oldest = moved(wide[count - 2 :], POSITION, 2) * keep_older.astype(BF16)
    wide = jnp.concatenate([oldest, previous, wide], axis=0)
    spread = jnp.pad(wide, ((0, 0), (0, 0), (0, 0), (1, 1)))
    spread = jnp.concatenate([spread[..., k : k + width] for k in range(3)], axis=2)
    taps = [spread[:, dr : dr + rows + 4] for dr in range(3)]
    taps.append(jnp.zeros(taps[0].shape[:2] + (SLOT - 27, width), BF16))
    taps = jnp.concatenate(taps, axis=2)

    win = jnp.pad(in_weight.reshape(3, 27, channels), ((0, 0), (0, SLOT - 27), (0, 0)))
    win = win.reshape(3 * SLOT, channels).T

    def side_by_side(weight):
        weight = weight.reshape(3, 3, 3, channels, channels)
        return weight.transpose(2, 4, 1, 0, 3).reshape(3 * channels, 9 * channels)

    cols = jnp.stack(
        [in_bias, gain_one, mid_bias, gain_two, out_bias, head_weight, in_bias, in_bias]
    )
    vmem = pl.BlockSpec(memory_space=pltpu.VMEM)
    features, weighted = pl.pallas_call(
        block_kernel,
        in_specs=[pl.BlockSpec(memory_space=pltpu.SMEM)] + [vmem] * 5,
        out_specs=[vmem, vmem],
        out_shape=[
            jax.ShapeDtypeStruct((rows, count, width * channels), BF16),
            jax.ShapeDtypeStruct((1, 128), F32),
        ],
        scratch_shapes=[
            pltpu.VMEM((rows + 4, count + 4, channels, width), BF16),
            pltpu.VMEM((rows + 2, count + 2, channels, width), BF16),
            pltpu.VMEM((rows + 4, count, channels, width), BF16),
            pltpu.VMEM((6, channels, width), F32),
            pltpu.VMEM((channels, width), F32),
            pltpu.VMEM((width, count, 128), F32),
        ],
        compiler_params=pltpu.CompilerParams(vmem_limit_bytes=56 << 20),
    )(flags, taps, win, side_by_side(mid_weight), side_by_side(out_weight), cols)
    features = features.transpose(1, 0, 2)

    labels = jnp.arange(targets.shape[0], dtype=jnp.int32)
    part = jnp.where(labels == clip_id, weighted[0, 0], 0.0)
    for axis in ("band", "span", "clip"):
        part = total_over(part, axis)
    member = (segments[:, None] == labels[None, :]).astype(F32)
    cells = jnp.sum(member, axis=0) * (count * rows * lax.axis_size("band") * width)
    scores = part / cells + head_bias[0]
    loss = jnp.mean((scores - targets) ** 2)
    return features, scores, loss


def solution(mesh):
    split = P(POSITION, "band", None)
    return jax.shard_map(
        local,
        mesh=mesh,
        in_specs=(split,) + (P(),) * 12,
        out_specs=(split, P(), P()),
        check_vma=False,
    )
```

profile of v0, /device:TPU:0, one launch (start us, length us, event | category | flops | bytes accessed | tf_op | source)
XLA Modules:
  0.0 104.0 jit_solution(6099117979456331581)
XLA Ops:
  0.6 0.0 copy-start.4
  0.6 0.0 copy-start.2
  0.7 0.0 copy-start
  0.7 1.4 %copy.25 = bf16[4,12,768]{1,0,2:T(4,128)(2,1)S(1)} copy(bf16[4,12,768]{2,0,1:T(4,128)(2,1)} %param.13) | data formatting | bytes 147456 | tf_op args[0]
  2.1 0.6 copy.26
  2.8 1.3 %collective-permute-start.1 = (bf16[4,3,3,256]{3,2,1,0:T(4,128)(2,1)S(1)}, bf16[4,3,3,256]{3,2,1,0:T(4,128)(2,1)S(1)}, u32[]{:S(2)}, u32[]{:S(2)}) collective-permute-start(bf16[4,3,3,256]{3,2,1,0:T(4,128)(2,1)S(1)} %get-tuple-element.15), channel_id=1, source_target_pairs={{1,0},{2,1},{3,2},{5,4},{6,5},{7,6},{9,8},{10,9},{11,10},{13,12},{... | collective-permute-start | bytes 55304 | tf_op jit(solution)/shard_map/ppermute | solution.py:19
  4.1 5.6 %collective-permute-start = (bf16[4,3,3,256]{3,2,1,0:T(4,128)(2,1)S(1)}, bf16[4,3,3,256]{3,2,1,0:T(4,128)(2,1)S(1)}, u32[]{:S(2)}, u32[]{:S(2)}) collective-permute-start(bf16[4,3,3,256]{3,2,1,0:T(4,128)(2,1)S(1)} %get-tuple-element.14), channel_id=1, source_target_pairs={{0,1},{1,2},{2,3},{4,5},{5,6},{6,7},{8,9},{9,10},{10,11},{12,13},{... | collective-permute-start | bytes 55304 | tf_op jit(solution)/shard_map/ppermute | solution.py:19
  9.6 0.0 copy-done.4
  9.7 0.1 convert_reduce_fusion
  9.8 0.7 fusion.10
  11.7 0.0 collective-permute-done.1
  11.7 0.0 collective-permute-done
  11.7 0.1 pad_maximum_fusion.1
  11.9 3.9 %collective-permute-start.2 = (bf16[2,18,3,256]{3,2,1,0:T(4,128)(2,1)S(1)}, bf16[2,18,3,256]{3,2,1,0:T(4,128)(2,1)S(1)}, u32[]{:S(2)}, u32[]{:S(2)}) collective-permute-start(bf16[2,18,3,256]{3,2,1,0:T(4,128)(2,1)S(1)} %slice.39), channel_id=1, source_target_pairs={{0,8},{4,12},{8,16},{12,20},{16,24},{20,28},{1,9},{5,13},{9,17},{1... | collective-permute-start | bytes 165896 | tf_op jit(solution)/shard_map/ppermute | solution.py:19
  15.8 0.6 pad_maximum_fusion.2.flags
  17.6 0.0 copy-done.2
  17.7 0.7 copy.29
  18.4 0.0 copy-done
  18.4 0.0 copy-start.1
  18.4 0.7 copy.30
  19.1 1.3 %reshape.32.wmid_ref = bf16[288,864]{1,0:T(8,128)(2,1)} reshape(bf16[3,96,3,3,96]{4,3,2,1,0:T(4,128)(2,1)S(1)} %bitcast.26) | data formatting | bytes 995328 | tf_op jit(solution)/shard_map/reshape | solution.py:161
  20.4 0.0 copy-done.1
  20.4 0.0 copy-start.3
  20.4 0.0 copy-start.5
  20.4 0.0 copy-start.6
  20.4 0.0 copy-start.7
  20.4 0.0 copy-start.8
  20.4 0.0 copy-start.9
  20.4 0.7 copy.31
  21.1 1.3 %reshape.34.wout_ref = bf16[288,864]{1,0:T(8,128)(2,1)} reshape(bf16[3,96,3,3,96]{4,3,2,1,0:T(4,128)(2,1)S(1)} %bitcast.27) | data formatting | bytes 995328 | tf_op jit(solution)/shard_map/reshape | solution.py:161
  23.0 0.1 pad.13.clone
  23.1 0.0 copy-done.3
  23.1 0.0 copy-done.5
  23.1 0.0 copy-done.6
  23.1 0.0 copy-done.7
  23.1 0.0 copy-done.8
  23.1 0.0 copy-done.9
  23.2 0.6 stack.53.cols_ref
  23.8 3.4 %collective-permute-start.3 = (bf16[4,18,3,256]{3,2,1,0:T(4,128)(2,1)S(1)}, bf16[4,18,3,256]{3,2,1,0:T(4,128)(2,1)S(1)}, u32[]{:S(2)}, u32[]{:S(2)}) collective-permute-start(bf16[4,18,3,256]{3,2,1,0:T(4,128)(2,1)S(1)} %pad_maximum_fusion.1), channel_id=1, source_target_pairs={{0,4},{4,8},{8,12},{12,16},{16,20},{20,24},{24,28},{1,5},{5,9},{9,... | collective-permute-start | bytes 331784 | tf_op jit(solution)/shard_map/ppermute | solution.py:19
  27.2 0.0 collective-permute-done.2
  27.2 2.6 %collective-permute-done.3 = bf16[4,18,3,256]{3,2,1,0:T(4,128)(2,1)S(1)} collective-permute-done((bf16[4,18,3,256]{3,2,1,0:T(4,128)(2,1)S(1)}, bf16[4,18,3,256]{3,2,1,0:T(4,128)(2,1)S(1)}, u32[]{:S(2)}, u32[]{:S(2)}) %collective-permute-start.3) | collective-permute-done | bytes 110624 | tf_op jit(solution)/shard_map/ppermute | solution.py:19
  29.8 0.1 broadcast_multiply_fusion
  29.9 0.5 fusion.1
  30.4 0.4 fusion.8
  30.8 0.9 pad_maximum_fusion
  31.7 0.4 fusion.7
  32.1 3.3 %maximum_maximum_fusion.x_ref = bf16[10,16,32,256]{3,2,1,0:T(8,128)(2,1)} fusion(bf16[10,16,9,256]{3,2,1,0:T(8,128)(2,1)S(1)} %get-tuple-element.10, bf16[10,16,9,256]{3,2,1,0:T(8,128)(2,1)S(1)} %get-tuple-element.11, bf16[10,16,9,256]{3,2,1,0:T(8,128)(2,1)S(1)} %get-tuple-element.9, bf16[32]{0:T(256)(128)(2,1)S(1)} %pad.13.clone), kind=kLoop, calls=%fused_computation | loop fusion | flops 10485760 | bytes 4833344 | tf_op jit(solution)/shard_map/concatenate | solution.py:154
  35.4 0.0 copy-start.10
  35.4 45.0 %shard_map.148 = (bf16[12,4,24576]{2,1,0:T(4,128)(2,1)}, f32[1,128]{1,0:T(1,128)}) custom-call(f32[3]{0:T(128)} %pad_maximum_fusion.2.flags, bf16[10,16,32,256]{3,2,1,0:T(8,128)(2,1)} %maximum_maximum_fusion.x_ref, bf16[96,96]{1,0:T(8,128)(2,1)} %bitcast.36, bf16[288,864]{1,0:T(8,128)(2,1)} %reshape.32.wmid_ref, bf16[288,864]{1,0:T(8,128)(2,1)} %reshape.34.wout_ref, ...), custom_call_target="tpu_custom_call" | custom-call | tf_op jit(solution)/shard_map/pallas_call | solution.py:167
  80.4 1.3 %compare_select_fusion = f32[4]{0:T(128)S(1)} fusion(f32[]{:T(128)} %bitcast.41, s32[]{:T(128)} %bitcast), kind=kLoop, calls=%fused_computation.16 | loop fusion | flops 8 | bytes 24 | tf_op jit(solution)/shard_map/jit(_where)/select_n | solution.py:188
  81.7 1.8 %collective-permute-start.4 = (f32[4]{0:T(128)S(1)}, f32[4]{0:T(128)S(1)}, u32[]{:S(2)}, u32[]{:S(2)}) collective-permute-start(f32[4]{0:T(128)S(1)} %compare_select_fusion), channel_id=1, source_target_pairs={{0,1},{1,0},{2,3},{3,2},{4,5},{5,4},{6,7},{7,6},{8,9},{9,8},{10,11... | collective-permute-start | bytes 56 | tf_op jit(solution)/shard_map/ppermute | solution.py:28
  83.5 1.8 %collective-permute-done.4 = f32[4]{0:T(128)S(1)} collective-permute-done((f32[4]{0:T(128)S(1)}, f32[4]{0:T(128)S(1)}, u32[]{:S(2)}, u32[]{:S(2)}) %collective-permute-start.4) | collective-permute-done | bytes 48 | tf_op jit(solution)/shard_map/ppermute | solution.py:28
  85.3 1.3 %fusion.11 = f32[4]{0:T(128)S(1)} fusion(f32[4]{0:T(128)S(1)} %collective-permute-done.4, f32[]{:T(128)} %bitcast.42, s32[]{:T(128)} %bitcast), kind=kLoop, calls=%fused_computation.25 | loop fusion | flops 12 | bytes 40 | tf_op jit(solution)/shard_map/add | solution.py:28
  86.6 2.8 %collective-permute-start.5 = (f32[4]{0:T(128)S(1)}, f32[4]{0:T(128)S(1)}, u32[]{:S(2)}, u32[]{:S(2)}) collective-permute-start(f32[4]{0:T(128)S(1)} %fusion.11), channel_id=1, source_target_pairs={{0,2},{1,3},{2,0},{3,1},{4,6},{5,7},{6,4},{7,5},{8,10},{9,11},{10,... | collective-permute-start | bytes 56 | tf_op jit(solution)/shard_map/ppermute | solution.py:28
  89.4 1.7 %collective-permute-done.5 = f32[4]{0:T(128)S(1)} collective-permute-done((f32[4]{0:T(128)S(1)}, f32[4]{0:T(128)S(1)}, u32[]{:S(2)}, u32[]{:S(2)}) %collective-permute-start.5) | collective-permute-done | bytes 48 | tf_op jit(solution)/shard_map/ppermute | solution.py:28
  91.1 1.3 %fusion.12 = f32[4]{0:T(128)S(1)} fusion(f32[4]{0:T(128)S(1)} %collective-permute-done.5, f32[4]{0:T(128)S(1)} %collective-permute-done.4, f32[]{:T(128)} %bitcast.43, s32[]{:T(128)} %bitcast), kind=kLoop, calls=%fused_computation.26 | loop fusion | flops 16 | bytes 56 | tf_op jit(solution)/shard_map/add | solution.py:28
  92.4 2.5 %collective-permute-start.6 = (f32[4]{0:T(128)S(1)}, f32[4]{0:T(128)S(1)}, u32[]{:S(2)}, u32[]{:S(2)}) collective-permute-start(f32[4]{0:T(128)S(1)} %fusion.12), channel_id=1, source_target_pairs={{0,4},{4,0},{8,12},{12,8},{1,5},{5,1},{9,13},{13,9},{2,6},{6,2},{1... | collective-permute-start | bytes 56 | tf_op jit(solution)/shard_map/ppermute | solution.py:28
  94.9 1.5 %collective-permute-done.6 = f32[4]{0:T(128)S(1)} collective-permute-done((f32[4]{0:T(128)S(1)}, f32[4]{0:T(128)S(1)}, u32[]{:S(2)}, u32[]{:S(2)}) %collective-permute-start.6) | collective-permute-done | bytes 48 | tf_op jit(solution)/shard_map/ppermute | solution.py:28
  96.5 1.5 %collective-permute-start.7 = (f32[4]{0:T(128)S(1)}, f32[4]{0:T(128)S(1)}, u32[]{:S(2)}, u32[]{:S(2)}) collective-permute-start(f32[4]{0:T(128)S(1)} %add.39), channel_id=1, source_target_pairs={{0,8},{4,12},{8,0},{12,4},{1,9},{5,13},{9,1},{13,5},{2,10},{6,14},... | collective-permute-start | bytes 56 | tf_op jit(solution)/shard_map/ppermute | solution.py:28
  97.9 2.1 %collective-permute-done.7 = f32[4]{0:T(128)S(1)} collective-permute-done((f32[4]{0:T(128)S(1)}, f32[4]{0:T(128)S(1)}, u32[]{:S(2)}, u32[]{:S(2)}) %collective-permute-start.7) | collective-permute-done | bytes 48 | tf_op jit(solution)/shard_map/ppermute | solution.py:28
  100.0 0.0 collective-permute-start.8
  100.0 1.1 %collective-permute-done.8 = f32[4]{0:T(128)S(1)} collective-permute-done((f32[4]{0:T(128)S(1)}, f32[4]{0:T(128)S(1)}, u32[]{:S(2)}, u32[]{:S(2)}) %collective-permute-start.8) | collective-permute-done | bytes 48 | tf_op jit(solution)/shard_map/ppermute | solution.py:28
  101.1 0.0 copy-done.10
  101.1 1.1 %multiply_reduce_fusion = (f32[]{:T(128)}, f32[4]{0:T(128)}) fusion(f32[4]{0:T(128)S(1)} %copy-done.10, f32[]{:T(128)} %bitcast.25, f32[4]{0:T(128)S(1)} %convert_reduce_fusion, f32[4]{0:T(128)S(1)} %add.40, f32[4]{0:T(128)S(1)} %collective-permute-done.8), kind=kLoop, calls=%fused_computation.18 | loop fusion | flops 27 | bytes 88 | tf_op jit(solution)/shard_map/reduce_sum | solution.py:194
  (9 shorter events, 0.1 us)
Async XLA Ops:
  0.6 9.0 %copy-start.4 = (s32[8]{0:T(128)S(1)}, s32[8]{0:T(128)}, u32[]{:S(2)}) copy-start(s32[8]{0:T(128)} %param.14) | copy-start | bytes 100
  0.6 17.0 %copy-start.2 = (bf16[3,3,9,96]{3,1,2,0:T(4,128)(2,1)S(1)}, bf16[3,3,9,96]{3,1,2,0:T(4,128)(2,1)}, u32[]{:S(2)}) copy-start(bf16[3,3,9,96]{3,1,2,0:T(4,128)(2,1)} %param.16) | copy-start | bytes 46660
  0.7 17.8 %copy-start = (bf16[3,3,288,96]{3,2,1,0:T(8,128)(2,1)S(1)}, bf16[3,3,288,96]{3,2,1,0:T(8,128)(2,1)}, u32[]{:S(2)}) copy-start(bf16[3,3,288,96]{3,2,1,0:T(8,128)(2,1)} %param.19) | copy-start | bytes 1492996
  2.8 8.9 %collective-permute-start.1 = (bf16[4,3,3,256]{3,2,1,0:T(4,128)(2,1)S(1)}, bf16[4,3,3,256]{3,2,1,0:T(4,128)(2,1)S(1)}, u32[]{:S(2)}, u32[]{:S(2)}) collective-permute-start(bf16[4,3,3,256]{3,2,1,0:T(4,128)(2,1)S(1)} %get-tuple-element.15), channel_id=1, source_target_pairs={{1,0},{2,1},{3,2},{5,4},{6,5},{7,6},{9,8},{10,9},{11,10},{13,12},{... | collective-permute-start | bytes 55304 | tf_op jit(solution)/shard_map/ppermute | solution.py:19
  4.1 7.7 %collective-permute-start = (bf16[4,3,3,256]{3,2,1,0:T(4,128)(2,1)S(1)}, bf16[4,3,3,256]{3,2,1,0:T(4,128)(2,1)S(1)}, u32[]{:S(2)}, u32[]{:S(2)}) collective-permute-start(bf16[4,3,3,256]{3,2,1,0:T(4,128)(2,1)S(1)} %get-tuple-element.14), channel_id=1, source_target_pairs={{0,1},{1,2},{2,3},{4,5},{5,6},{6,7},{8,9},{9,10},{10,11},{12,13},{... | collective-permute-start | bytes 55304 | tf_op jit(solution)/shard_map/ppermute | solution.py:19
  11.9 15.3 %collective-permute-start.2 = (bf16[2,18,3,256]{3,2,1,0:T(4,128)(2,1)S(1)}, bf16[2,18,3,256]{3,2,1,0:T(4,128)(2,1)S(1)}, u32[]{:S(2)}, u32[]{:S(2)}) collective-permute-start(bf16[2,18,3,256]{3,2,1,0:T(4,128)(2,1)S(1)} %slice.39), channel_id=1, source_target_pairs={{0,8},{4,12},{8,16},{12,20},{16,24},{20,28},{1,9},{5,13},{9,17},{1... | collective-permute-start | bytes 165896 | tf_op jit(solution)/shard_map/ppermute | solution.py:19
  18.4 2.0 %copy-start.1 = (bf16[3,3,288,96]{3,2,1,0:T(8,128)(2,1)S(1)}, bf16[3,3,288,96]{3,2,1,0:T(8,128)(2,1)}, u32[]{:S(2)}) copy-start(bf16[3,3,288,96]{3,2,1,0:T(8,128)(2,1)} %param.22) | copy-start | bytes 1492996
  20.4 2.8 %copy-start.3 = (f32[96]{0:T(128)S(1)}, f32[96]{0:T(128)}, u32[]{:S(2)}) copy-start(f32[96]{0:T(128)} %param.17) | copy-start | bytes 1156
  20.4 2.8 %copy-start.5 = (f32[96]{0:T(128)S(1)}, f32[96]{0:T(128)}, u32[]{:S(2)}) copy-start(f32[96]{0:T(128)} %param.18) | copy-start | bytes 1156
  20.4 2.8 %copy-start.6 = (f32[96]{0:T(128)S(1)}, f32[96]{0:T(128)}, u32[]{:S(2)}) copy-start(f32[96]{0:T(128)} %param.20) | copy-start | bytes 1156
  20.4 2.8 %copy-start.7 = (f32[96]{0:T(128)S(1)}, f32[96]{0:T(128)}, u32[]{:S(2)}) copy-start(f32[96]{0:T(128)} %param.21) | copy-start | bytes 1156
  20.4 2.7 %copy-start.8 = (f32[96]{0:T(128)S(1)}, f32[96]{0:T(128)}, u32[]{:S(2)}) copy-start(f32[96]{0:T(128)} %param.23) | copy-start | bytes 1156
  20.4 2.7 %copy-start.9 = (f32[96]{0:T(128)S(1)}, f32[96]{0:T(128)}, u32[]{:S(2)}) copy-start(f32[96]{0:T(128)} %param.24) | copy-start | bytes 1156
  23.8 6.0 %collective-permute-start.3 = (bf16[4,18,3,256]{3,2,1,0:T(4,128)(2,1)S(1)}, bf16[4,18,3,256]{3,2,1,0:T(4,128)(2,1)S(1)}, u32[]{:S(2)}, u32[]{:S(2)}) collective-permute-start(bf16[4,18,3,256]{3,2,1,0:T(4,128)(2,1)S(1)} %pad_maximum_fusion.1), channel_id=1, source_target_pairs={{0,4},{4,8},{8,12},{12,16},{16,20},{20,24},{24,28},{1,5},{5,9},{9,... | collective-permute-start | bytes 331784 | tf_op jit(solution)/shard_map/ppermute | solution.py:19
  35.4 65.7 %copy-start.10 = (f32[4]{0:T(128)S(1)}, f32[4]{0:T(128)}, u32[]{:S(2)}) copy-start(f32[4]{0:T(128)} %param.15) | copy-start | bytes 52
  81.7 3.6 %collective-permute-start.4 = (f32[4]{0:T(128)S(1)}, f32[4]{0:T(128)S(1)}, u32[]{:S(2)}, u32[]{:S(2)}) collective-permute-start(f32[4]{0:T(128)S(1)} %compare_select_fusion), channel_id=1, source_target_pairs={{0,1},{1,0},{2,3},{3,2},{4,5},{5,4},{6,7},{7,6},{8,9},{9,8},{10,11... | collective-permute-start | bytes 56 | tf_op jit(solution)/shard_map/ppermute | solution.py:28
  86.6 4.5 %collective-permute-start.5 = (f32[4]{0:T(128)S(1)}, f32[4]{0:T(128)S(1)}, u32[]{:S(2)}, u32[]{:S(2)}) collective-permute-start(f32[4]{0:T(128)S(1)} %fusion.11), channel_id=1, source_target_pairs={{0,2},{1,3},{2,0},{3,1},{4,6},{5,7},{6,4},{7,5},{8,10},{9,11},{10,... | collective-permute-start | bytes 56 | tf_op jit(solution)/shard_map/ppermute | solution.py:28
  92.4 4.1 %collective-permute-start.6 = (f32[4]{0:T(128)S(1)}, f32[4]{0:T(128)S(1)}, u32[]{:S(2)}, u32[]{:S(2)}) collective-permute-start(f32[4]{0:T(128)S(1)} %fusion.12), channel_id=1, source_target_pairs={{0,4},{4,0},{8,12},{12,8},{1,5},{5,1},{9,13},{13,9},{2,6},{6,2},{1... | collective-permute-start | bytes 56 | tf_op jit(solution)/shard_map/ppermute | solution.py:28
  96.5 3.5 %collective-permute-start.7 = (f32[4]{0:T(128)S(1)}, f32[4]{0:T(128)S(1)}, u32[]{:S(2)}, u32[]{:S(2)}) collective-permute-start(f32[4]{0:T(128)S(1)} %add.39), channel_id=1, source_target_pairs={{0,8},{4,12},{8,0},{12,4},{1,9},{5,13},{9,1},{13,5},{2,10},{6,14},... | collective-permute-start | bytes 56 | tf_op jit(solution)/shard_map/ppermute | solution.py:28
  100.0 1.1 %collective-permute-start.8 = (f32[4]{0:T(128)S(1)}, f32[4]{0:T(128)S(1)}, u32[]{:S(2)}, u32[]{:S(2)}) collective-permute-start(f32[4]{0:T(128)S(1)} %add.40), channel_id=1, source_target_pairs={{0,16},{16,0},{1,17},{17,1},{2,18},{18,2},{3,19},{19,3},{4,20},{20... | collective-permute-start | bytes 56 | tf_op jit(solution)/shard_map/ppermute | solution.py:28
where the time goes:
time: 104 us
  Pallas kernels  45 us (43%)
  starting transfers between devices  22.7 us (22%)
  waiting for transfers between devices  10.9 us (10%)
  other arithmetic  10.6 us (10%)
  local copies, waits for them, and re-layouts  8.91 us (9%)
  between operations  5.96 us (6%)
    pallas_call x1, Pallas kernels, local(): pl.pallas_call(block_kernel, in_specs=[pl.BlockSpec(memory_space=pltpu.SM...  45 us
    ppermute x4, starting transfers between devices, moved(): return lax.ppermute(block, axis, route)  14.1 us
    ppermute x5, starting transfers between devices, total_over(): lax.ppermute(value, axis, [(i, i ^ step) for i in range(count)])  8.56 us
    ppermute x5, waiting for transfers between devices, total_over(): lax.ppermute(value, axis, [(i, i ^ step) for i in range(count)])  8.27 us
    concatenate x1, other arithmetic, local(): taps = jnp.concatenate(taps, axis=2)  3.29 us
    ppermute x4, waiting for transfers between devices, moved(): return lax.ppermute(block, axis, route)  2.6 us
    reshape x2, local copies, waits for them, and re-layouts, side_by_side(): return weight.transpose(2, 4, 1, 0, 3).reshape(3 * channels, 9 * channels)  2.6 us
    add x4, other arithmetic, total_over(): value + lax.ppermute(value, axis, [(i, i ^ step) for i in range(count)])  2.56 us
  transfers between devices with their start and end apart: 9, of which 6 were waited for; matrix products, arithmetic and copies ran while one was open for 6% of the time, Pallas kernels for 0%

commit v1 on v0

v1 whole, which is shorter than its diff:
```python
import jax
import jax.numpy as jnp
from jax import lax
from jax.experimental import pallas as pl
from jax.experimental.pallas import tpu as pltpu
from jax.sharding import PartitionSpec as P

BF16 = jnp.bfloat16
F32 = jnp.float32
POSITION = ("clip", "span")
EVERY = ("clip", "span", "band")
SLOT = 16
SPAN_SLOTS = 16


def moved(block, axis, distance):
    count = lax.axis_size(axis)
    route = [(i, i + distance) for i in range(count) if 0 <= i + distance < count]
    return lax.ppermute(block, axis, route)


def shifted_sum(product, channels, first, last):
    width = product.shape[1]
    left = jnp.where(first, 0.0, pltpu.roll(product[:channels], 1, 1))
    right = jnp.where(last, 0.0, pltpu.roll(product[2 * channels :], width - 1, 1))
    return product[channels : 2 * channels] + left + right


def rms_silu(value, gain):
    scale = lax.rsqrt(jnp.mean(value * value, axis=0, keepdims=True) + 1e-06)
    half = value * scale * (0.5 * gain)
    return half + half * jnp.tanh(half)


def block_kernel(
    seg_ref, x_ref, win_ref, wmid_ref, wout_ref, cols_ref, out_ref, sum_ref,
    planes, inputs, win, wmid, wout, act_one, act_two, h0_ref, table, total, stage,
):
    rows, count = out_ref.shape[0], out_ref.shape[1]
    channels = cols_ref.shape[1]
    width = inputs.shape[3]
    pairs = width // 2
    position, band = lax.axis_index(POSITION), lax.axis_index("band")
    clip_id = seg_ref[position]
    before = seg_ref[jnp.maximum(position - 1, 0)]
    older = seg_ref[jnp.maximum(position - 2, 0)]
    keep = jnp.where((position > 0) & (clip_id == before), 1.0, 0.0)
    keep_older = jnp.where((position > 1) & (older == before), keep, 0.0)
    top = jnp.where(band > 0, 1.0, 0.0)
    bottom = jnp.where(band < lax.axis_size("band") - 1, 1.0, 0.0)

    unit = jnp.where(
        lax.broadcasted_iota(jnp.int32, (channels, channels), 0)
        == lax.broadcasted_iota(jnp.int32, (channels, channels), 1), 1.0, 0.0,
    ).astype(BF16)

    def turned(weight):
        return lax.dot_general(
            unit, weight, (((1,), (1,)), ((), ())), preferred_element_type=F32
        ).astype(BF16)

    for source, target in ((wmid_ref, wmid), (wout_ref, wout)):
        for k in range(3):
            piece = [
                source[dt, dr, k * channels : (k + 1) * channels]
                for dr in range(3) for dt in range(3)
            ]
            target[k * channels : (k + 1) * channels] = turned(jnp.concatenate(piece, axis=0))
    win[...] = turned(win_ref[...])
    columns = jnp.transpose(cols_ref[...])
    for j in range(6):
        table[j] = jnp.broadcast_to(columns[:, j : j + 1], (channels, width))
    total[...] = jnp.zeros_like(total)

    span = 3 * pairs
    lane = lax.broadcasted_iota(jnp.int32, (span, span), 1)
    pick = lax.broadcasted_iota(jnp.int32, (span, span), 0) == 3 * (lane % pairs) + lane // pairs
    pick = jnp.where(pick, 1.0, 0.0).astype(BF16)
    frames = x_ref.shape[0] * x_ref.shape[1]
    flat = x_ref[...].reshape(frames, x_ref.shape[2])
    halves = [
        jnp.dot(flat[:, h * span : (h + 1) * span], pick, preferred_element_type=F32)
        for h in range(2)
    ]
    slot = lax.broadcasted_iota(jnp.int32, (frames, width), 0) % SPAN_SLOTS
    kept = jnp.where(slot < 2, keep_older, jnp.where(slot < 6, keep, 1.0))
    pixel = lax.broadcasted_iota(jnp.int32, (frames, width), 1)
    for c in range(3):
        plane = jnp.concatenate([h[:, c * pairs : (c + 1) * pairs] for h in halves], axis=1) * kept
        planes[:, c, :] = jnp.where(pixel == 0, 0.0, pltpu.roll(plane, 1, 1))
        planes[:, 3 + c, :] = plane
        planes[:, 6 + c, :] = jnp.where(pixel == width - 1, 0.0, pltpu.roll(plane, width - 1, 1))
    for c in range(9, SLOT):
        planes[:, c, :] = jnp.zeros((frames, width), F32)

    def narrow(row, carry):
        at = pl.multiple_of(row * SPAN_SLOTS, SPAN_SLOTS)
        inputs[row] = planes[pl.ds(at, SPAN_SLOTS)].astype(BF16)
        return carry

    lax.fori_loop(0, rows + 6, narrow, 0)

    pixel = lax.broadcasted_iota(jnp.int32, (channels, width), 1)
    first, last = pixel == 0, pixel == width - 1

    def row_mask(row, rim, extent):
        inside = jnp.where(row < rim, top, 1.0)
        return inside * jnp.where(row >= extent - rim, bottom, 1.0)

    def taps_of(source, row, t):
        depth = 3 * source.shape[2]
        return jnp.concatenate(
            [source[row + dr, t : t + 3].reshape(depth, width) for dr in range(3)], axis=0
        )

    def first_row(row):
        mask = row_mask(row, 2, rows + 4)
        for t in range(count + 4):
            h0 = jnp.dot(win[...], taps_of(inputs, row, t), preferred_element_type=F32)
            h0 = (h0 + table[0]).astype(BF16)
            if t >= 4:
                h0_ref[row, t - 4] = h0
            act = rms_silu(h0.astype(F32), table[1]) * (mask * keep if t < 4 else mask)
            act_one[row, t] = act.astype(BF16)

    def middle_row(row):
        mask = row_mask(row, 1, rows + 2)
        for t in range(count + 2):
            product = jnp.dot(wmid[...], taps_of(act_one, row, t), preferred_element_type=F32)
            h1 = shifted_sum(product, channels, first, last) + table[2]
            act = rms_silu(h1, table[3]) * (mask * keep if t < 2 else mask)
            act_two[row, t] = act.astype(BF16)

    def last_row(row):
        for t in range(count):
            product = jnp.dot(wout[...], taps_of(act_two, row, t), preferred_element_type=F32)
            value = shifted_sum(product, channels, first, last) + table[4]
            value = (value + h0_ref[row + 2, t].astype(F32)).astype(BF16).astype(F32)
            total[...] += value
            padded = jnp.concatenate([value, jnp.zeros((128 - channels, width), F32)], axis=0)
            stage[:, t, :] = jnp.transpose(padded)

    lanes = lax.broadcasted_iota(jnp.int32, (width // 4, count, 128), 2)

    def written(row):
        pixels = stage[...].reshape(width // 4, 4, count, 128)
        one = pltpu.roll(pixels[:, 1], 96, 2)
        two = pltpu.roll(pixels[:, 2], 64, 2)
        three = pltpu.roll(pixels[:, 3], 32, 2)
        tiles = [
            jnp.where(lanes < 96, pixels[:, 0], one).astype(BF16),
            jnp.where(lanes < 64, one, two).astype(BF16),
            jnp.where(lanes < 32, two, three).astype(BF16),
        ]
        for group in range(width // 4):
            for j in range(3):
                at = (3 * group + j) * 128
                out_ref[row, :, at : at + 128] = tiles[j][group]

    def loop(begin, end, *steps):
        def body(row, carry):
            for step, lag in steps:
                step(row + lag)
            return carry

        lax.fori_loop(begin, end, body, 0)

    loop(0, 3, (first_row, 0))
    loop(0, 3, (first_row, 3), (middle_row, 0))
    written_before = lambda row: written(jnp.maximum(row - 1, 0))
    loop(0, rows - 2, (written_before, 0), (first_row, 6), (last_row, 0), (middle_row, 3))
    loop(rows - 2, rows - 1, (written_before, 0), (last_row, 0), (middle_row, 3))
    loop(rows - 1, rows, (written_before, 0), (last_row, 0))
    written(rows - 1)
    clip = lax.broadcasted_iota(jnp.int32, sum_ref.shape, 1)
    weighted = jnp.sum(total[...] * table[5], keepdims=True)
    sum_ref[...] = jnp.where(clip == clip_id, jnp.broadcast_to(weighted, sum_ref.shape), 0.0)


def local(
    frames, segments, targets, in_weight, in_bias, gain_one, mid_weight, mid_bias,
    gain_two, out_weight, out_bias, head_weight, head_bias,
):
    count, rows = frames.shape[0], frames.shape[1]
    channels = in_bias.shape[0]
    width = frames.shape[2] // 3
    devices = lax.axis_size(EVERY)

    own = frames.transpose(1, 0, 2)
    low = moved(own[rows - 3 :], "band", 1)
    high = moved(own[:3], "band", -1)
    wide = jnp.concatenate([low, own, high], axis=0)
    previous = moved(wide, POSITION, 1)
    oldest = moved(wide[:, count - 2 :], POSITION, 2)
    unused = jnp.zeros((rows + 6, SPAN_SLOTS - 2 * count - 2, 3 * width), BF16)
    seen = jnp.concatenate([oldest, previous, wide, unused], axis=1)

    win = jnp.pad(in_weight, ((0, 0), (0, 0), (0, SLOT - 9), (0, 0)))
    win = win.transpose(1, 0, 2, 3).reshape(9 * SLOT, channels)
    cols = jnp.stack(
        [in_bias, gain_one, mid_bias, gain_two, out_bias, head_weight, in_bias, in_bias]
    )
    vmem = pl.BlockSpec(memory_space=pltpu.VMEM)
    features, weighted = pl.pallas_call(
        block_kernel,
        in_specs=[pl.BlockSpec(memory_space=pltpu.SMEM)] + [vmem] * 5,
        out_specs=[vmem, vmem],
        out_shape=[
            jax.ShapeDtypeStruct((rows, count, width * channels), BF16),
            jax.ShapeDtypeStruct((devices, 128), F32),
        ],
        scratch_shapes=[
            pltpu.VMEM(((rows + 6) * SPAN_SLOTS, SLOT, width), F32),
            pltpu.VMEM((rows + 6, SPAN_SLOTS, SLOT, width), BF16),
            pltpu.VMEM((channels, 9 * SLOT), BF16),
            pltpu.VMEM((3 * channels, 9 * channels), BF16),
            pltpu.VMEM((3 * channels, 9 * channels), BF16),
            pltpu.VMEM((rows + 4, count + 4, channels, width), BF16),
            pltpu.VMEM((rows + 2, count + 2, channels, width), BF16),
            pltpu.VMEM((rows + 4, count, channels, width), BF16),
            pltpu.VMEM((6, channels, width), F32),
            pltpu.VMEM((channels, width), F32),
            pltpu.VMEM((width, count, 128), F32),
        ],
        compiler_params=pltpu.CompilerParams(vmem_limit_bytes=56 << 20),
    )(segments, seen, win, mid_weight, out_weight, cols)
    features = features.transpose(1, 0, 2)

    clips = targets.shape[0]
    gathered = lax.all_to_all(weighted, EVERY, 0, 0, tiled=True)
    part = jnp.sum(gathered[:, :clips], axis=0)
    labels = jnp.arange(clips, dtype=jnp.int32)
    member = (segments[:, None] == labels[None, :]).astype(F32)
    cells = jnp.sum(member, axis=0) * (count * rows * lax.axis_size("band") * width)
    scores = part / cells + head_bias[0]
    loss = jnp.mean((scores - targets) ** 2)
    return features, scores, loss


def solution(mesh):
    split = P(POSITION, "band", None)
    return jax.shard_map(
        local,
        mesh=mesh,
        in_specs=(split,) + (P(),) * 12,
        out_specs=(split, P(), P()),
        check_vma=False,
    )
```

time: 104 us -> 77.2 us (0.74)
  Pallas kernels: 45 us -> 38.2 us
  other arithmetic: 10.6 us -> 4.22 us
  starting transfers between devices: 22.7 us -> 16.7 us
  local copies, waits for them, and re-layouts: 8.91 us -> 3.68 us
  between operations: 5.96 us -> 3.14 us
    ppermute x5 -> x0, starting transfers between devices: 8.56 us -> none  [total_over(): lax.ppermute(value, axis, [(i, i ^ step) for i in range(count)])]
    ppermute x5 -> x0, waiting for transfers between devices: 8.27 us -> none  [total_over(): lax.ppermute(value, axis, [(i, i ^ step) for i in range(count)])]
    pallas_call x1, Pallas kernels: 45 us -> 38.2 us  [local(): pl.pallas_call(block_kernel, in_specs=[pl.BlockSpec(memory_space=pltpu.SM...]
    all_to_all x0 -> x1, waiting for transfers between devices: none -> 6.35 us  [local(): gathered = lax.all_to_all(weighted, EVERY, 0, 0, tiled=True)]
    reshape x6 -> x0, local copies, waits for them, and re-layouts: 5.25 us -> none  [the longest x2 2.6 us: side_by_side(): return weight.transpose(2, 4, 1, 0, 3).reshape(3 * channels, 9 * channels)]
    all_to_all x0 -> x1, starting transfers between devices: none -> 3.67 us  [local(): gathered = lax.all_to_all(weighted, EVERY, 0, 0, tiled=True)]
    add x4 -> x0, other arithmetic: 2.56 us -> none  [total_over(): value + lax.ppermute(value, axis, [(i, i ^ step) for i in range(count)])]
    concatenate x4 -> x2, other arithmetic: 4.85 us -> 2.9 us  [the longest x1 1.93 us: local(): seen = jnp.concatenate([oldest, previous, wide, unused], axis=1)]
  transfers between devices with their start and end apart: 9 -> 5, of which waited for: 6 -> 3; matrix products, arithmetic and copies ran while one was open for 6% -> 4% of each run, Pallas kernels for 0% -> 0%
where the time goes in v1:
time: 77.2 us; the launch traced here: 76.7 us
  Pallas kernels  38.2 us (49%)
  starting transfers between devices  16.7 us (22%)
  waiting for transfers between devices  10.7 us (14%)
  other arithmetic  4.22 us (5%)
  local copies, waits for them, and re-layouts  3.68 us (5%)
  between operations  3.14 us (4%)
    pallas_call x1, Pallas kernels, local(): pl.pallas_call(block_kernel, in_specs=[pl.BlockSpec(memory_space=pltpu.SM...  38.2 us
    ppermute x4, starting transfers between devices, moved(): return lax.ppermute(block, axis, route)  13 us
    all_to_all x1, waiting for transfers between devices, local(): gathered = lax.all_to_all(weighted, EVERY, 0, 0, tiled=True)  6.35 us
    ppermute x4, waiting for transfers between devices, moved(): return lax.ppermute(block, axis, route)  4.36 us
    all_to_all x1, starting transfers between devices, local(): gathered = lax.all_to_all(weighted, EVERY, 0, 0, tiled=True)  3.67 us
    concatenate x1, other arithmetic, local(): seen = jnp.concatenate([oldest, previous, wide, unused], axis=1)  1.93 us
  transfers between devices with their start and end apart: 5, of which 3 were waited for; matrix products, arithmetic and copies ran while one was open for 4% of the time, Pallas kernels for 0%

profile of v1, /device:TPU:0, one launch (start us, length us, event | category | flops | bytes accessed | tf_op | source)
XLA Modules:
  0.0 76.7 jit_solution(17569954746165421777)
XLA Ops:
  0.6 0.0 copy-start.1
  0.6 0.0 copy-start
  0.7 0.8 fusion.2
  1.4 4.9 %collective-permute-start = (bf16[3,4,768]{2,1,0:T(4,128)(2,1)S(1)}, bf16[3,4,768]{2,1,0:T(4,128)(2,1)S(1)}, u32[]{:S(2)}, u32[]{:S(2)}) collective-permute-start(bf16[3,4,768]{2,1,0:T(4,128)(2,1)S(1)} %get-tuple-element.9), channel_id=1, source_target_pairs={{0,1},{1,2},{2,3},{4,5},{5,6},{6,7},{8,9},{9,10},{10,11},{12,13},{... | collective-permute-start | bytes 55304 | tf_op jit(solution)/shard_map/ppermute | solution.py:19
  6.4 1.3 %collective-permute-start.1 = (bf16[3,4,768]{2,1,0:T(4,128)(2,1)S(1)}, bf16[3,4,768]{2,1,0:T(4,128)(2,1)S(1)}, u32[]{:S(2)}, u32[]{:S(2)}) collective-permute-start(bf16[3,4,768]{2,1,0:T(4,128)(2,1)S(1)} %get-tuple-element.10), channel_id=1, source_target_pairs={{1,0},{2,1},{3,2},{5,4},{6,5},{7,6},{9,8},{10,9},{11,10},{13,12},{... | collective-permute-start | bytes 55304 | tf_op jit(solution)/shard_map/ppermute | solution.py:19
  7.7 0.1 collective-permute-done
  7.8 4.2 %collective-permute-done.1 = bf16[3,4,768]{2,1,0:T(4,128)(2,1)S(1)} collective-permute-done((bf16[3,4,768]{2,1,0:T(4,128)(2,1)S(1)}, bf16[3,4,768]{2,1,0:T(4,128)(2,1)S(1)}, u32[]{:S(2)}, u32[]{:S(2)}) %collective-permute-start.1) | collective-permute-done | bytes 18464 | tf_op jit(solution)/shard_map/ppermute | solution.py:19
  12.0 1.0 %pad_maximum_fusion = bf16[18,4,768]{2,1,0:T(4,128)(2,1)S(1)} fusion(bf16[3,4,768]{2,1,0:T(4,128)(2,1)S(1)} %collective-permute-done.1, bf16[12,4,768]{2,1,0:T(4,128)(2,1)} %bitcast.18, bf16[3,4,768]{2,1,0:T(4,128)(2,1)S(1)} %collective-permute-done), kind=kLoop, calls=%fused_computation.1 | loop fusion | flops 110592 | bytes 221184 | tf_op jit(solution)/shard_map/concatenate | solution.py:192
  13.0 0.1 slice.18
  13.1 3.4 %collective-permute-start.3 = (bf16[18,4,768]{2,1,0:T(4,128)(2,1)S(1)}, bf16[18,4,768]{2,1,0:T(4,128)(2,1)S(1)}, u32[]{:S(2)}, u32[]{:S(2)}) collective-permute-start(bf16[18,4,768]{2,1,0:T(4,128)(2,1)S(1)} %pad_maximum_fusion), channel_id=1, source_target_pairs={{0,4},{4,8},{8,12},{12,16},{16,20},{20,24},{24,28},{1,5},{5,9},{9,... | collective-permute-start | bytes 331784 | tf_op jit(solution)/shard_map/ppermute | solution.py:19
  16.5 3.4 %collective-permute-start.2 = (bf16[18,2,768]{2,1,0:T(2,128)(2,1)S(1)}, bf16[18,2,768]{2,1,0:T(2,128)(2,1)S(1)}, u32[]{:S(2)}, u32[]{:S(2)}) collective-permute-start(bf16[18,2,768]{2,1,0:T(2,128)(2,1)S(1)} %slice.18), channel_id=1, source_target_pairs={{0,8},{4,12},{8,16},{12,20},{16,24},{20,28},{1,9},{5,13},{9,17},{1... | collective-permute-start | bytes 165896 | tf_op jit(solution)/shard_map/ppermute | solution.py:19
  19.9 0.8 %pad_bitcast_fusion = bf16[3,3,16,96]{3,0,2,1:T(4,128)(2,1)S(1)} fusion(bf16[3,3,9,96]{3,1,2,0:T(4,128)(2,1)} %param.16), kind=kLoop, calls=%fused_computation.2 | loop fusion | bytes 43200 | tf_op jit(solution)/shard_map/transpose | solution.py:199
  20.7 0.6 copy.19
  21.3 0.1 pad.10.clone
  21.4 1.4 %stack.29.cols_ref = f32[8,96]{1,0:T(8,128)} concatenate(f32[1,96]{1,0:T(1,128)} %bitcast.23, f32[1,96]{1,0:T(1,128)} %bitcast.26, f32[1,96]{1,0:T(1,128)} %bitcast.27, f32[1,96]{1,0:T(1,128)} %bitcast.28, f32[1,96]{1,0:T(1,128)} %bitcast.29, f32[1,96]{1,0:T(1,128)} %bitcast.30, f32[1,96]{1,0:T(1,128)} %bitcast.24, f32[1,96]{1,0:T(1,128)} %bitcast.25), dimensions={0} | concatenate | bytes 6144 | tf_op jit(solution)/shard_map/stack | solution.py:200
  22.7 0.0 collective-permute-done.2
  22.7 0.0 collective-permute-done.3
  22.7 1.9 %maximum_maximum_fusion.x_ref = bf16[18,16,768]{2,1,0:T(8,128)(2,1)} fusion(bf16[3,4,768]{2,1,0:T(4,128)(2,1)S(1)} %collective-permute-done.1, bf16[12,4,768]{2,1,0:T(4,128)(2,1)} %bitcast.19, bf16[3,4,768]{2,1,0:T(4,128)(2,1)S(1)} %collective-permute-done, bf16[18,4,768]{2,1,0:T(4,128)(2,1)S(1)} %collective-permute-done.3, ...), kind=kLoop, calls=%fused_computation | loop fusion | flops 2654208 | bytes 718880 | tf_op jit(solution)/shard_map/concatenate | solution.py:196
  24.7 38.2 %shard_map.148 = (bf16[12,4,24576]{2,1,0:T(4,128)(2,1)}, f32[32,128]{1,0:T(8,128)}) custom-call(s32[8]{0:T(128)} %seg_ref.1, bf16[18,16,768]{2,1,0:T(8,128)(2,1)} %maximum_maximum_fusion.x_ref, bf16[144,96]{1,0:T(8,128)(2,1)} %bitcast.20, bf16[3,3,288,96]{3,2,1,0:T(8,128)(2,1)} %wmid_ref.1, bf16[3,3,288,96]{3,2,1,0:T(8,128)(2,1)} %wout_ref.1, ...), custom_call_target="tpu_custom_call" | custom-call | tf_op jit(solution)/shard_map/pallas_call | solution.py:204
  62.9 3.7 %all-to-all-start = ((f32[32,1,128]{2,1,0:T(1,128)}), f32[32,1,128]{2,1,0:T(1,128)S(1)}, u32[]{:S(2)}, u32[]{:S(2)}) async-start(f32[32,1,128]{2,1,0:T(1,128)} %bitcast.22), calls=%async_computation | async-start | bytes 32768 | tf_op jit(solution)/shard_map/all_to_all | solution.py:230
  66.6 0.0 copy-done.1
  66.6 0.1 convert_reduce_fusion
  67.4 6.3 %all-to-all-done = f32[32,1,128]{2,1,0:T(1,128)S(1)} async-done(((f32[32,1,128]{2,1,0:T(1,128)}), f32[32,1,128]{2,1,0:T(1,128)S(1)}, u32[]{:S(2)}, u32[]{:S(2)}) %all-to-all-start) | async-done | bytes 16416 | tf_op jit(solution)/shard_map/all_to_all | solution.py:230
  73.7 0.0 copy-done
  73.7 1.2 %multiply_reduce_fusion = (f32[]{:T(128)}, f32[4]{0:T(128)}) fusion(f32[4]{0:T(128)S(1)} %copy-done, f32[]{:T(128)} %bitcast.16, f32[4]{0:T(128)S(1)} %slice_reduce_fusion, f32[4]{0:T(128)S(1)} %convert_reduce_fusion), kind=kLoop, calls=%fused_computation.6 | loop fusion | flops 23 | bytes 72 | tf_op jit(solution)/shard_map/reduce_sum | solution.py:236
  (2 shorter events, 0.0 us)
Async XLA Ops:
  0.6 66.0 %copy-start.1 = (s32[8]{0:T(128)S(1)}, s32[8]{0:T(128)}, u32[]{:S(2)}) copy-start(s32[8]{0:T(128)} %seg_ref.1) | copy-start | bytes 100
  0.6 73.1 %copy-start = (f32[4]{0:T(128)S(1)}, f32[4]{0:T(128)}, u32[]{:S(2)}) copy-start(f32[4]{0:T(128)} %param.15) | copy-start | bytes 52
  1.4 6.4 %collective-permute-start = (bf16[3,4,768]{2,1,0:T(4,128)(2,1)S(1)}, bf16[3,4,768]{2,1,0:T(4,128)(2,1)S(1)}, u32[]{:S(2)}, u32[]{:S(2)}) collective-permute-start(bf16[3,4,768]{2,1,0:T(4,128)(2,1)S(1)} %get-tuple-element.9), channel_id=1, source_target_pairs={{0,1},{1,2},{2,3},{4,5},{5,6},{6,7},{8,9},{9,10},{10,11},{12,13},{... | collective-permute-start | bytes 55304 | tf_op jit(solution)/shard_map/ppermute | solution.py:19
  6.4 5.7 %collective-permute-start.1 = (bf16[3,4,768]{2,1,0:T(4,128)(2,1)S(1)}, bf16[3,4,768]{2,1,0:T(4,128)(2,1)S(1)}, u32[]{:S(2)}, u32[]{:S(2)}) collective-permute-start(bf16[3,4,768]{2,1,0:T(4,128)(2,1)S(1)} %get-tuple-element.10), channel_id=1, source_target_pairs={{1,0},{2,1},{3,2},{5,4},{6,5},{7,6},{9,8},{10,9},{11,10},{13,12},{... | collective-permute-start | bytes 55304 | tf_op jit(solution)/shard_map/ppermute | solution.py:19
  13.1 9.7 %collective-permute-start.3 = (bf16[18,4,768]{2,1,0:T(4,128)(2,1)S(1)}, bf16[18,4,768]{2,1,0:T(4,128)(2,1)S(1)}, u32[]{:S(2)}, u32[]{:S(2)}) collective-permute-start(bf16[18,4,768]{2,1,0:T(4,128)(2,1)S(1)} %pad_maximum_fusion), channel_id=1, source_target_pairs={{0,4},{4,8},{8,12},{12,16},{16,20},{20,24},{24,28},{1,5},{5,9},{9,... | collective-permute-start | bytes 331784 | tf_op jit(solution)/shard_map/ppermute | solution.py:19
  16.5 6.3 %collective-permute-start.2 = (bf16[18,2,768]{2,1,0:T(2,128)(2,1)S(1)}, bf16[18,2,768]{2,1,0:T(2,128)(2,1)S(1)}, u32[]{:S(2)}, u32[]{:S(2)}) collective-permute-start(bf16[18,2,768]{2,1,0:T(2,128)(2,1)S(1)} %slice.18), channel_id=1, source_target_pairs={{0,8},{4,12},{8,16},{12,20},{16,24},{20,28},{1,9},{5,13},{9,17},{1... | collective-permute-start | bytes 165896 | tf_op jit(solution)/shard_map/ppermute | solution.py:19
  62.9 10.8 %all-to-all-start = ((f32[32,1,128]{2,1,0:T(1,128)}), f32[32,1,128]{2,1,0:T(1,128)S(1)}, u32[]{:S(2)}, u32[]{:S(2)}) async-start(f32[32,1,128]{2,1,0:T(1,128)} %bitcast.22), calls=%async_computation | async-start | bytes 32768 | tf_op jit(solution)/shard_map/all_to_all | solution.py:230

commit v2 on v1

v2 whole, which is shorter than its diff:
```python
import functools

import jax
import jax.numpy as jnp
from jax import lax
from jax.experimental import pallas as pl
from jax.experimental.pallas import tpu as pltpu
from jax.sharding import PartitionSpec as P

BF16 = jnp.bfloat16
F32 = jnp.float32
POSITION = ("clip", "span")
EVERY = ("clip", "span", "band")
SLOTS = 8


def moved(block, axis, distance):
    count = lax.axis_size(axis)
    route = [(i, i + distance) for i in range(count) if 0 <= i + distance < count]
    return lax.ppermute(block, axis, route)


def shifted_sum(product, channels):
    left, middle, right = (product[k * channels : (k + 1) * channels] for k in range(3))
    lane = lax.broadcasted_iota(jnp.int32, (channels, 128), 1)
    tiles = product.shape[1] // 128
    cut = [slice(i * 128, (i + 1) * 128) for i in range(tiles)]
    left = [pltpu.roll(left[:, c], 1, 1) for c in cut]
    right = [pltpu.roll(right[:, c], 127, 1) for c in cut]
    parts = []
    for i in range(tiles):
        low = jnp.where(lane == 0, left[i - 1] if i else 0.0, left[i])
        high = jnp.where(lane == 127, right[i + 1] if i + 1 < tiles else 0.0, right[i])
        parts.append(middle[:, cut[i]] + low + high)
    return jnp.concatenate(parts, axis=1)


def rms_silu(value, half_gain, mask):
    scale = lax.rsqrt(jnp.mean(value * value, axis=0, keepdims=True) + 1e-06) * mask
    half = value * scale * half_gain
    return half + half * jnp.tanh(half)


def pipelined(units):
    waiting = []
    for start, ends in units:
        product = start()
        for end in waiting:
            end()
        waiting = [functools.partial(end, product) for end in ends]
    for end in waiting:
        end()


def block_kernel(
    seg_ref, own_ref, previous_ref, oldest_ref, low_ref, high_ref,
    win_ref, wmid_ref, wout_ref, cols_ref, out_ref, sum_ref,
    gathered, planes, win, wmid, wout, act_one, act_two, h0_ref, table, total, stage, order,
    tiles_ref,
):
    rows, count = out_ref.shape[0], out_ref.shape[1]
    channels = cols_ref.shape[1]
    width = own_ref.shape[2] // 3
    pairs = width // 2
    position, band = lax.axis_index(POSITION), lax.axis_index("band")
    clip_id = seg_ref[position]
    before = seg_ref[jnp.maximum(position - 1, 0)]
    older = seg_ref[jnp.maximum(position - 2, 0)]
    keep = jnp.where((position > 0) & (clip_id == before), 1.0, 0.0)
    keep_older = jnp.where((position > 1) & (older == before), keep, 0.0)
    top = jnp.where(band > 0, 1.0, 0.0)
    bottom = jnp.where(band < lax.axis_size("band") - 1, 1.0, 0.0)

    unit = jnp.where(
        lax.broadcasted_iota(jnp.int32, (channels, channels), 0)
        == lax.broadcasted_iota(jnp.int32, (channels, channels), 1), 1.0, 0.0,
    ).astype(BF16)

    def turned(weight):
        return lax.dot_general(
            unit, weight, (((1,), (1,)), ((), ())), preferred_element_type=F32
        ).astype(BF16)

    for source, target in ((wmid_ref, wmid), (wout_ref, wout)):
        for k in range(3):
            piece = [
                source[dt, dr, k * channels : (k + 1) * channels]
                for dr in range(3) for dt in range(3)
            ]
            target[k * channels : (k + 1) * channels] = turned(jnp.concatenate(piece, axis=0))
    bias = cols_ref[:1]
    high = bias.astype(BF16).astype(F32)
    middle = (bias - high).astype(BF16).astype(F32)
    low = bias - high - middle
    bias = jnp.concatenate([high, middle, low, jnp.zeros((5, channels), F32)], axis=0)
    for t in range(count):
        piece = pltpu.roll(win_ref[...], t, 1) if t else win_ref[...]
        piece = jnp.concatenate([piece.reshape(27 * SLOTS, channels), bias], axis=0)
        win[t * channels : (t + 1) * channels] = turned(piece.astype(BF16))
    columns = jnp.transpose(cols_ref[...])
    for j in range(6):
        column = columns[:, j : j + 1] * (0.5 if j in (1, 3) else 1.0)
        table[j] = jnp.broadcast_to(column, (channels, width))
    total[...] = jnp.zeros_like(total)

    span = 3 * pairs
    lane = lax.broadcasted_iota(jnp.int32, (span, span), 1)
    pick = lax.broadcasted_iota(jnp.int32, (span, span), 0) == 3 * (lane % pairs) + lane // pairs
    pick = jnp.where(pick, 1.0, 0.0).astype(BF16)
    sources = ((0, oldest_ref, 6, 2, 4), (2, previous_ref, 3, 0, 4), (6, own_ref, 0, 0, 2),
               (8, previous_ref, 3, 2, 4), (10, own_ref, 0, 0, 4))
    for at, source, rim, begin, end in sources:
        to = slice(at, at + end - begin)
        gathered[3 : rows + 3, to] = source[:, begin:end].astype(F32)
        gathered[:3, to] = low_ref[rim : rim + 3, begin:end].astype(F32)
        gathered[rows + 3 :, to] = high_ref[rim : rim + 3, begin:end].astype(F32)
    gathered[:, 14:] = jnp.zeros((rows + 6, 2, 3 * width), F32)
    frames = (rows + 6) * 2 * SLOTS
    flat = gathered[...].reshape(frames, 3 * width).astype(BF16)
    halves = [
        jnp.dot(flat[:, h * span : (h + 1) * span], pick, preferred_element_type=F32)
        for h in range(2)
    ]
    slot = lax.broadcasted_iota(jnp.int32, (frames, width), 0) % (2 * SLOTS)
    kept = jnp.where((slot < 6) | (slot == 8) | (slot == 9), keep, 1.0)
    kept = jnp.where(slot < 2, keep_older, kept)
    pixel = lax.broadcasted_iota(jnp.int32, (frames, width), 1)
    for c in range(3):
        plane = jnp.concatenate([h[:, c * pairs : (c + 1) * pairs] for h in halves], axis=1) * kept
        planes[c] = jnp.where(pixel == 0, 0.0, pltpu.roll(plane, 1, 1)).reshape(planes.shape[1:])
        planes[3 + c] = plane.reshape(planes.shape[1:])
        plane = jnp.where(pixel == width - 1, 0.0, pltpu.roll(plane, width - 1, 1))
        planes[6 + c] = plane.reshape(planes.shape[1:])

    part = width // 4
    row = lax.broadcasted_iota(jnp.int32, (width, width), 0)
    pixel = row % part // count * 4 + row // part
    wanted = row % count * part + pixel
    hit = lax.broadcasted_iota(jnp.int32, (width, width), 1) == wanted
    order[...] = jnp.where(hit, 1.0, 0.0).astype(BF16)
    stage[...] = jnp.zeros_like(stage)

    def row_mask(row, rim, extent):
        inside = jnp.where(row < rim, top, 1.0)
        return inside * jnp.where(row >= extent - rim, bottom, 1.0)

    def taps_of(source, row, t):
        return jnp.concatenate(
            [source[row + dr, t : t + 3].reshape(3 * channels, width) for dr in range(3)], axis=0
        )

    def first_units(row):
        mask = row_mask(row, 2, rows + 4)

        def end(t, at, product):
            h0 = product[at : at + channels].astype(BF16)
            if t >= 4:
                h0_ref[row, t - 4] = h0
            act = rms_silu(h0.astype(F32), table[1], mask * keep if t < 4 else mask)
            act_one[row, t] = act.astype(BF16)

        def start(half):
            taps = planes[:, pl.ds(row, 3), half * SLOTS : (half + 1) * SLOTS]
            taps = [taps.reshape(27 * SLOTS, width), jnp.ones((SLOTS, width), F32)]
            taps = jnp.concatenate(taps, axis=0).astype(BF16)
            return jnp.dot(win[...], taps, preferred_element_type=F32)

        return [
            (
                functools.partial(start, half),
                [functools.partial(end, count * half + t, t * channels) for t in range(count)],
            )
            for half in range(2)
        ]

    def middle_units(row):
        mask = row_mask(row, 1, rows + 2)

        def start(t):
            return jnp.dot(wmid[...], taps_of(act_one, row, t), preferred_element_type=F32)

        def end(t, product):
            h1 = shifted_sum(product, channels) + table[2]
            act = rms_silu(h1, table[3], mask * keep if t < 2 else mask)
            act_two[row, t] = act.astype(BF16)

        return [
            (functools.partial(start, t), [functools.partial(end, t)]) for t in range(count + 2)
        ]

    def last_units(row):
        def start(t):
            return jnp.dot(wout[...], taps_of(act_two, row, t), preferred_element_type=F32)

        def end(t, product):
            value = shifted_sum(product, channels) + table[4]
            value = (value + h0_ref[row + 2, t].astype(F32)).astype(BF16)
            total[...] += value.astype(F32)
            stage[t, :channels] = value

        return [(functools.partial(start, t), [functools.partial(end, t)]) for t in range(count)]

    def written_units():
        lane = lax.broadcasted_iota(jnp.int32, (128, 128), 1)

        def start(piece):
            half = slice(piece // 2 * 128, piece // 2 * 128 + 128)
            sides = []
            for t in range(0, count, 2):
                one, two = stage[t, :, half].astype(F32), stage[t + 1, :, half].astype(F32)
                if piece % 2:
                    one = pltpu.roll(one, part, 1)
                else:
                    two = pltpu.roll(two, part, 1)
                sides.append(jnp.where(lane < part, one, two).astype(BF16))
            return lax.dot_general(
                order[...], jnp.concatenate(sides, axis=1), (((1,), (1,)), ((), ())),
                preferred_element_type=F32,
            )

        def end(piece, product):
            pixels = [product[i * part : (i + 1) * part] for i in range(4)]
            pixels = [pltpu.roll(x, 128 - 32 * i, 1) if i else x for i, x in enumerate(pixels)]
            lane = lax.broadcasted_iota(jnp.int32, (part, 128), 1)
            for j in range(3):
                tile = jnp.where(lane < 96 - 32 * j, pixels[j], pixels[j + 1])
                for group in range(part // count):
                    at = (3 * (piece * part // count + group) + j) * 128
                    tiles_ref[:, at : at + 128] = tile[group * count : (group + 1) * count]

        return [
            (functools.partial(start, piece), [functools.partial(end, piece)])
            for piece in range(4)
        ]

    def written(row):
        out_ref[row] = tiles_ref[...].astype(BF16)

    def mixed(first, second):
        units = []
        for i in range(max(len(first), len(second))):
            units += first[i : i + 1] + second[i : i + 1]
        return units

    def loop(begin, end, body):
        def step(row, carry):
            body(row)
            return carry

        lax.fori_loop(begin, end, step, 0)

    loop(0, 3, lambda row: pipelined(first_units(row)))
    loop(0, 3, lambda row: pipelined(mixed(middle_units(row), first_units(row + 3))))

    def steady(row, middle=True, first=True):
        units = mixed(written_units(), middle_units(row + 3) if middle else [])
        units += mixed(last_units(row), first_units(row + 6) if first else [])
        pipelined(units)
        written(jnp.maximum(row - 1, 0))

    loop(0, rows - 2, steady)
    loop(rows - 2, rows - 1, lambda row: steady(row, first=False))
    loop(rows - 1, rows, lambda row: steady(row, middle=False, first=False))
    pipelined(written_units())
    written(rows - 1)
    clip = lax.broadcasted_iota(jnp.int32, sum_ref.shape, 1)
    weighted = jnp.sum(total[...] * table[5], keepdims=True)
    sum_ref[...] = jnp.where(clip == clip_id, jnp.broadcast_to(weighted, sum_ref.shape), 0.0)


def local(
    frames, segments, targets, in_weight, in_bias, gain_one, mid_weight, mid_bias,
    gain_two, out_weight, out_bias, head_weight, head_bias,
):
    count, rows = frames.shape[0], frames.shape[1]
    channels = in_bias.shape[0]
    width = frames.shape[2] // 3
    devices = lax.axis_size(EVERY)

    own = frames.transpose(1, 0, 2)
    previous = moved(own, POSITION, 1)
    oldest = moved(own, POSITION, 2)
    spans = (own, previous, oldest)
    low = moved(jnp.concatenate([x[rows - 3 :] for x in spans], axis=0), "band", 1)
    high = moved(jnp.concatenate([x[:3] for x in spans], axis=0), "band", -1)

    win = in_weight.transpose(2, 1, 0, 3).reshape(27, 3, channels).astype(F32)
    win = jnp.pad(win, ((0, 0), (0, SLOTS - 3), (0, 0)))
    cols = jnp.stack(
        [in_bias, gain_one, mid_bias, gain_two, out_bias, head_weight, in_bias, in_bias]
    )
    vmem = pl.BlockSpec(memory_space=pltpu.VMEM)
    features, weighted = pl.pallas_call(
        block_kernel,
        in_specs=[pl.BlockSpec(memory_space=pltpu.SMEM)] + [vmem] * 9,
        out_specs=[vmem, vmem],
        out_shape=[
            jax.ShapeDtypeStruct((rows, count, width * channels), BF16),
            jax.ShapeDtypeStruct((devices, 128), F32),
        ],
        scratch_shapes=[
            pltpu.VMEM((rows + 6, 2 * SLOTS, 3 * width), F32),
            pltpu.VMEM((9, rows + 6, 2 * SLOTS, width), F32),
            pltpu.VMEM((count * channels, 28 * SLOTS), BF16),
            pltpu.VMEM((3 * channels, 9 * channels), BF16),
            pltpu.VMEM((3 * channels, 9 * channels), BF16),
            pltpu.VMEM((rows + 4, count + 4, channels, width), BF16),
            pltpu.VMEM((rows + 2, count + 2, channels, width), BF16),
            pltpu.VMEM((rows + 4, count, channels, width), BF16),
            pltpu.VMEM((6, channels, width), F32),
            pltpu.VMEM((channels, width), F32),
            pltpu.VMEM((count, 128, width), BF16),
            pltpu.VMEM((width, width), BF16),
            pltpu.VMEM((count, width * channels), F32),
        ],
        compiler_params=pltpu.CompilerParams(vmem_limit_bytes=56 << 20),
    )(segments, own, previous, oldest, low, high, win, mid_weight, out_weight, cols)
    features = features.transpose(1, 0, 2)

    clips = targets.shape[0]
    gathered = lax.all_to_all(weighted, EVERY, 0, 0, tiled=True)
    part = jnp.sum(gathered[:, :clips], axis=0)
    labels = jnp.arange(clips, dtype=jnp.int32)
    member = (segments[:, None] == labels[None, :]).astype(F32)
    cells = jnp.sum(member, axis=0) * (count * rows * lax.axis_size("band") * width)
    scores = part / cells + head_bias[0]
    loss = jnp.mean((scores - targets) ** 2)
    return features, scores, loss


def solution(mesh):
    split = P(POSITION, "band", None)
    return jax.shard_map(
        local,
        mesh=mesh,
        in_specs=(split,) + (P(),) * 12,
        out_specs=(split, P(), P()),
        check_vma=False,
    )
```

time: 77.2 us -> 72.7 us (0.942)
  Pallas kernels: 38.2 us -> 35.8 us
  other arithmetic: 4.22 us -> 2.08 us
  starting transfers between devices: 16.7 us -> 17.8 us
  waiting for transfers between devices: 10.7 us -> 9.74 us
    concatenate x2, other arithmetic: 2.9 us -> 0.09 us  [the longest x1 0.04 us: local(): jnp.concatenate([x[rows - 3:] for x in spans], axis=0)]
    pallas_call x1, Pallas kernels: 38.2 us -> 35.8 us  [local(): pl.pallas_call(block_kernel, in_specs=[pl.BlockSpec(memory_space=pltpu.SM...]
    transpose x2 -> x0, local copies, waits for them, and re-layouts: 1.39 us -> none  [local(): win = win.transpose(1, 0, 2, 3).reshape(9 * SLOT, channels)]
    all_to_all x1, starting transfers between devices: 3.67 us -> 4.66 us  [local(): gathered = lax.all_to_all(weighted, EVERY, 0, 0, tiled=True)]
    ppermute x4, waiting for transfers between devices: 4.36 us -> 3.39 us  [moved(): return lax.ppermute(block, axis, route)]
  transfers between devices with their start and end apart: 5 -> 5, of which waited for: 3 -> 3; matrix products, arithmetic and copies ran while one was open for 4% -> 5% of each run, Pallas kernels for 0% -> 0%
where the time goes in v2:
time: 72.7 us; the launch traced here: 72.3 us
  Pallas kernels  35.8 us (49%)
  starting transfers between devices  17.8 us (24%)
  waiting for transfers between devices  9.74 us (13%)
  local copies, waits for them, and re-layouts  3.58 us (5%)
  between operations  3.23 us (4%)
  other arithmetic  2.08 us (3%)
    pallas_call x1, Pallas kernels, local(): pl.pallas_call(block_kernel, in_specs=[pl.BlockSpec(memory_space=pltpu.SM...  35.8 us
    ppermute x4, starting transfers between devices, moved(): return lax.ppermute(block, axis, route)  13.2 us
    all_to_all x1, waiting for transfers between devices, local(): gathered = lax.all_to_all(weighted, EVERY, 0, 0, tiled=True)  6.35 us
    all_to_all x1, starting transfers between devices, local(): gathered = lax.all_to_all(weighted, EVERY, 0, 0, tiled=True)  4.66 us
    ppermute x4, waiting for transfers between devices, moved(): return lax.ppermute(block, axis, route)  3.39 us
  transfers between devices with their start and end apart: 5, of which 3 were waited for; matrix products, arithmetic and copies ran while one was open for 5% of the time, Pallas kernels for 0%

profile of v2, /device:TPU:0, one launch (start us, length us, event | category | flops | bytes accessed | tf_op | source)
XLA Modules:
  0.0 72.3 jit_solution(1221183315835194095)
XLA Ops:
  0.6 0.0 copy-start.5
  0.6 0.0 copy-start.4
  0.7 5.0 %collective-permute-start = (bf16[12,4,768]{2,1,0:T(4,128)(2,1)}, bf16[12,4,768]{2,1,0:T(4,128)(2,1)S(1)}, u32[]{:S(2)}, u32[]{:S(2)}) collective-permute-start(bf16[12,4,768]{2,1,0:T(4,128)(2,1)} %bitcast.16), channel_id=1, source_target_pairs={{0,4},{4,8},{8,12},{12,16},{16,20},{20,24},{24,28},{1,5},{5,9},{9,... | collective-permute-start | bytes 221192 | tf_op jit(solution)/shard_map/ppermute | solution.py:20
  5.6 3.4 %collective-permute-start.1 = (bf16[12,4,768]{2,1,0:T(4,128)(2,1)}, bf16[12,4,768]{2,1,0:T(4,128)(2,1)S(1)}, u32[]{:S(2)}, u32[]{:S(2)}) collective-permute-start(bf16[12,4,768]{2,1,0:T(4,128)(2,1)} %bitcast.17), channel_id=1, source_target_pairs={{0,8},{4,12},{8,16},{12,20},{16,24},{20,28},{1,9},{5,13},{9,17},{1... | collective-permute-start | bytes 221192 | tf_op jit(solution)/shard_map/ppermute | solution.py:20
  9.1 0.8 %fusion.2 = (bf16[3,4,768]{2,1,0:T(4,128)(2,1)S(1)}, bf16[3,4,768]{2,1,0:T(4,128)(2,1)S(1)}) fusion(bf16[12,4,768]{2,1,0:T(4,128)(2,1)} %bitcast.18), kind=kLoop, calls=%fused_computation.9 | loop fusion | bytes 73728 | tf_op jit(solution)/shard_map/slice | solution.py:285
  9.9 0.8 %copy.19 = bf16[9,3,3,96]{3,2,1,0:T(4,128)(2,1)S(1)} copy(bf16[9,3,3,96]{3,1,0,2:T(4,128)(2,1)} %bitcast.22) | data formatting | bytes 31104 | tf_op jit(solution)/shard_map/convert_element_type | solution.py:287
  10.6 0.0 collective-permute-done.previous_ref
  10.6 0.0 copy-start
  10.7 0.7 collective-permute-done.1.oldest_ref
  11.4 0.0 copy-start.1
  11.4 3.5 %collective-permute-start.2 = (bf16[9,4,768]{2,1,0:T(4,128)(2,1)S(1)}, bf16[9,4,768]{2,1,0:T(4,128)(2,1)S(1)}, u32[]{:S(2)}, u32[]{:S(2)}) collective-permute-start(bf16[9,4,768]{2,1,0:T(4,128)(2,1)S(1)} %pad_maximum_fusion), channel_id=1, source_target_pairs={{0,1},{1,2},{2,3},{4,5},{5,6},{6,7},{8,9},{9,10},{10,11},{12,13},{... | collective-permute-start | bytes 165896 | tf_op jit(solution)/shard_map/ppermute | solution.py:20
  15.0 1.3 %collective-permute-start.3 = (bf16[9,4,768]{2,1,0:T(4,128)(2,1)S(1)}, bf16[9,4,768]{2,1,0:T(4,128)(2,1)S(1)}, u32[]{:S(2)}, u32[]{:S(2)}) collective-permute-start(bf16[9,4,768]{2,1,0:T(4,128)(2,1)S(1)} %pad_maximum_fusion.1), channel_id=1, source_target_pairs={{1,0},{2,1},{3,2},{5,4},{6,5},{7,6},{9,8},{10,9},{11,10},{13,12},{... | collective-permute-start | bytes 165896 | tf_op jit(solution)/shard_map/ppermute | solution.py:20
  16.3 0.7 pad_convert_fusion.win_ref
  16.9 1.4 %stack.29.cols_ref = f32[8,96]{1,0:T(8,128)} concatenate(f32[1,96]{1,0:T(1,128)} %bitcast.24, f32[1,96]{1,0:T(1,128)} %bitcast.27, f32[1,96]{1,0:T(1,128)} %bitcast.28, f32[1,96]{1,0:T(1,128)} %bitcast.29, f32[1,96]{1,0:T(1,128)} %bitcast.30, f32[1,96]{1,0:T(1,128)} %bitcast.31, f32[1,96]{1,0:T(1,128)} %bitcast.25, f32[1,96]{1,0:T(1,128)} %bitcast.26), dimensions={0} | concatenate | bytes 6144 | tf_op jit(solution)/shard_map/stack | solution.py:289
  18.3 0.0 collective-permute-done.2.low_ref
  18.3 0.0 copy-start.2
  18.3 2.7 %collective-permute-done.3.high_ref = bf16[9,4,768]{2,1,0:T(4,128)(2,1)S(1)} collective-permute-done((bf16[9,4,768]{2,1,0:T(4,128)(2,1)S(1)}, bf16[9,4,768]{2,1,0:T(4,128)(2,1)S(1)}, u32[]{:S(2)}, u32[]{:S(2)}) %collective-permute-start.3) | collective-permute-done | bytes 55328 | tf_op jit(solution)/shard_map/ppermute | solution.py:20
  21.0 0.0 copy-done
  21.0 0.0 copy-done.1
  21.0 0.0 copy-done.2
  21.0 0.0 copy-start.3
  21.0 0.6 copy-done.3
  21.6 35.8 %shard_map.148 = (bf16[12,4,24576]{2,1,0:T(4,128)(2,1)}, f32[32,128]{1,0:T(8,128)}) custom-call(s32[8]{0:T(128)} %seg_ref.1, bf16[12,4,768]{2,1,0:T(4,128)(2,1)} %bitcast.19, bf16[12,4,768]{2,1,0:T(4,128)(2,1)} %copy-done, bf16[12,4,768]{2,1,0:T(4,128)(2,1)} %copy-done.1, bf16[9,4,768]{2,1,0:T(4,128)(2,1)} %copy-done.2, bf16[9,4,768]{2,1,0:T(4,128)(2,1)} %copy-done.3, ...), custom_call_target="tpu_custom_call" | custom-call | tf_op jit(solution)/shard_map/pallas_call | solution.py:293
  57.4 4.7 %all-to-all-start = ((f32[32,1,128]{2,1,0:T(1,128)}), f32[32,1,128]{2,1,0:T(1,128)S(1)}, u32[]{:S(2)}, u32[]{:S(2)}) async-start(f32[32,1,128]{2,1,0:T(1,128)} %bitcast.23), calls=%async_computation | async-start | bytes 32768 | tf_op jit(solution)/shard_map/all_to_all | solution.py:321
  62.1 0.0 copy-done.5
  62.1 0.1 convert_reduce_fusion
  62.9 6.3 %all-to-all-done = f32[32,1,128]{2,1,0:T(1,128)S(1)} async-done(((f32[32,1,128]{2,1,0:T(1,128)}), f32[32,1,128]{2,1,0:T(1,128)S(1)}, u32[]{:S(2)}, u32[]{:S(2)}) %all-to-all-start) | async-done | bytes 16416 | tf_op jit(solution)/shard_map/all_to_all | solution.py:321
  69.3 0.0 copy-done.4
  69.3 1.2 %multiply_reduce_fusion = (f32[]{:T(128)}, f32[4]{0:T(128)}) fusion(f32[4]{0:T(128)S(1)} %copy-done.4, f32[]{:T(128)} %bitcast.15, f32[4]{0:T(128)S(1)} %slice_reduce_fusion, f32[4]{0:T(128)S(1)} %convert_reduce_fusion), kind=kLoop, calls=%fused_computation.6 | loop fusion | flops 23 | bytes 72 | tf_op jit(solution)/shard_map/reduce_sum | solution.py:327
  (5 shorter events, 0.1 us)
Async XLA Ops:
  0.6 61.5 %copy-start.5 = (s32[8]{0:T(128)S(1)}, s32[8]{0:T(128)}, u32[]{:S(2)}) copy-start(s32[8]{0:T(128)} %seg_ref.1) | copy-start | bytes 100
  0.6 68.6 %copy-start.4 = (f32[4]{0:T(128)S(1)}, f32[4]{0:T(128)}, u32[]{:S(2)}) copy-start(f32[4]{0:T(128)} %param.15) | copy-start | bytes 52
  0.7 10.0 %collective-permute-start = (bf16[12,4,768]{2,1,0:T(4,128)(2,1)}, bf16[12,4,768]{2,1,0:T(4,128)(2,1)S(1)}, u32[]{:S(2)}, u32[]{:S(2)}) collective-permute-start(bf16[12,4,768]{2,1,0:T(4,128)(2,1)} %bitcast.16), channel_id=1, source_target_pairs={{0,4},{4,8},{8,12},{12,16},{16,20},{20,24},{24,28},{1,5},{5,9},{9,... | collective-permute-start | bytes 221192 | tf_op jit(solution)/shard_map/ppermute | solution.py:20
  5.6 5.7 %collective-permute-start.1 = (bf16[12,4,768]{2,1,0:T(4,128)(2,1)}, bf16[12,4,768]{2,1,0:T(4,128)(2,1)S(1)}, u32[]{:S(2)}, u32[]{:S(2)}) collective-permute-start(bf16[12,4,768]{2,1,0:T(4,128)(2,1)} %bitcast.17), channel_id=1, source_target_pairs={{0,8},{4,12},{8,16},{12,20},{16,24},{20,28},{1,9},{5,13},{9,17},{1... | collective-permute-start | bytes 221192 | tf_op jit(solution)/shard_map/ppermute | solution.py:20
  10.6 10.4 %copy-start = (bf16[12,4,768]{2,1,0:T(4,128)(2,1)}, bf16[12,4,768]{2,1,0:T(4,128)(2,1)S(1)}, u32[]{:S(2)}) copy-start(bf16[12,4,768]{2,1,0:T(4,128)(2,1)S(1)} %collective-permute-done.previous_ref) | copy-start | bytes 221188
  11.4 9.7 %copy-start.1 = (bf16[12,4,768]{2,1,0:T(4,128)(2,1)}, bf16[12,4,768]{2,1,0:T(4,128)(2,1)S(1)}, u32[]{:S(2)}) copy-start(bf16[12,4,768]{2,1,0:T(4,128)(2,1)S(1)} %collective-permute-done.1.oldest_ref) | copy-start | bytes 221188
  11.4 6.9 %collective-permute-start.2 = (bf16[9,4,768]{2,1,0:T(4,128)(2,1)S(1)}, bf16[9,4,768]{2,1,0:T(4,128)(2,1)S(1)}, u32[]{:S(2)}, u32[]{:S(2)}) collective-permute-start(bf16[9,4,768]{2,1,0:T(4,128)(2,1)S(1)} %pad_maximum_fusion), channel_id=1, source_target_pairs={{0,1},{1,2},{2,3},{4,5},{5,6},{6,7},{8,9},{9,10},{10,11},{12,13},{... | collective-permute-start | bytes 165896 | tf_op jit(solution)/shard_map/ppermute | solution.py:20
  15.0 6.0 %collective-permute-start.3 = (bf16[9,4,768]{2,1,0:T(4,128)(2,1)S(1)}, bf16[9,4,768]{2,1,0:T(4,128)(2,1)S(1)}, u32[]{:S(2)}, u32[]{:S(2)}) collective-permute-start(bf16[9,4,768]{2,1,0:T(4,128)(2,1)S(1)} %pad_maximum_fusion.1), channel_id=1, source_target_pairs={{1,0},{2,1},{3,2},{5,4},{6,5},{7,6},{9,8},{10,9},{11,10},{13,12},{... | collective-permute-start | bytes 165896 | tf_op jit(solution)/shard_map/ppermute | solution.py:20
  18.3 2.7 %copy-start.2 = (bf16[9,4,768]{2,1,0:T(4,128)(2,1)}, bf16[9,4,768]{2,1,0:T(4,128)(2,1)S(1)}, u32[]{:S(2)}) copy-start(bf16[9,4,768]{2,1,0:T(4,128)(2,1)S(1)} %collective-permute-done.2.low_ref) | copy-start | bytes 165892
  21.0 0.6 copy-start.3
  57.4 11.8 %all-to-all-start = ((f32[32,1,128]{2,1,0:T(1,128)}), f32[32,1,128]{2,1,0:T(1,128)S(1)}, u32[]{:S(2)}, u32[]{:S(2)}) async-start(f32[32,1,128]{2,1,0:T(1,128)} %bitcast.23), calls=%async_computation | async-start | bytes 32768 | tf_op jit(solution)/shard_map/all_to_all | solution.py:321

commit v3 on v2

--- a/solution.py
+++ b/solution.py
@@ -52,24 +52,32 @@
         end()
 
 
-def block_kernel(
-    seg_ref, own_ref, previous_ref, oldest_ref, low_ref, high_ref,
-    win_ref, wmid_ref, wout_ref, cols_ref, out_ref, sum_ref,
-    gathered, planes, win, wmid, wout, act_one, act_two, h0_ref, table, total, stage, order,
-    tiles_ref,
+def prepared_kernel(
+    win_ref, wmid_ref, wout_ref, cols_ref,
+    flags, win, table, mid_alone, mid_both, mid_rest, out_alone, out_both, out_rest,
 ):
-    rows, count = out_ref.shape[0], out_ref.shape[1]
-    channels = cols_ref.shape[1]
-    width = own_ref.shape[2] // 3
-    pairs = width // 2
+    width, channels = table.shape[2], cols_ref.shape[1]
+    count = win.shape[0] // channels
+    mid_parts = mid_alone, mid_both, mid_rest
+    out_parts = out_alone, out_both, out_rest
+
     position, band = lax.axis_index(POSITION), lax.axis_index("band")
-    clip_id = seg_ref[position]
-    before = seg_ref[jnp.maximum(position - 1, 0)]
-    older = seg_ref[jnp.maximum(position - 2, 0)]
+    place = lax.broadcasted_iota(jnp.int32, (1, channels), 1)
+
+    def clip_at(index):
+        chosen = jnp.where(place == index, cols_ref[6:7], 0.0)
+        return jnp.sum(chosen, axis=1, keepdims=True)
+
+    clip_id, before, older = clip_at(position), clip_at(position - 1), clip_at(position - 2)
     keep = jnp.where((position > 0) & (clip_id == before), 1.0, 0.0)
     keep_older = jnp.where((position > 1) & (older == before), keep, 0.0)
     top = jnp.where(band > 0, 1.0, 0.0)
     bottom = jnp.where(band < lax.axis_size("band") - 1, 1.0, 0.0)
+    for i, flag in enumerate((keep, keep_older, top, bottom)):
+        flags[i : i + 1] = jnp.broadcast_to(flag, (1, width))
+    clip = lax.broadcasted_iota(jnp.int32, (1, width), 1)
+    flags[4:5] = jnp.where(clip.astype(F32) == clip_id, 1.0, 0.0)
+    flags[5:] = jnp.zeros((3, width), F32)
 
     unit = jnp.where(
         lax.broadcasted_iota(jnp.int32, (channels, channels), 0)
@@ -81,13 +89,27 @@
             unit, weight, (((1,), (1,)), ((), ())), preferred_element_type=F32
         ).astype(BF16)
 
-    for source, target in ((wmid_ref, wmid), (wout_ref, wout)):
+    block = 3 * channels
+    begin = block // 256 * 256
+    end = 3 * block // 256 * 256 + 256
+    for source, (alone, both, rest) in ((wmid_ref, mid_parts), (wout_ref, out_parts)):
         for k in range(3):
-            piece = [
-                source[dt, dr, k * channels : (k + 1) * channels]
-                for dr in range(3) for dt in range(3)
-            ]
-            target[k * channels : (k + 1) * channels] = turned(jnp.concatenate(piece, axis=0))
+            piece = jnp.concatenate(
+                [
+                    source[dr, dt, k * channels : (k + 1) * channels]
+                    for dr in range(3) for dt in range(3)
+                ],
+                axis=0,
+            )
+            at = slice(k * channels, (k + 1) * channels)
+            beside = slice(block + k * channels, block + (k + 1) * channels)
+            none = jnp.zeros((end - 3 * block, channels), BF16)
+            alone[at] = turned(piece[:begin])
+            both[at] = turned(jnp.concatenate([piece[begin:], none], axis=0))
+            none = jnp.zeros((block - begin, channels), BF16)
+            both[beside] = turned(jnp.concatenate([none, piece[: end - block]], axis=0))
+            rest[at] = turned(piece[end - block :])
+
     bias = cols_ref[:1]
     high = bias.astype(BF16).astype(F32)
     middle = (bias - high).astype(BF16).astype(F32)
@@ -101,6 +123,22 @@
     for j in range(6):
         column = columns[:, j : j + 1] * (0.5 if j in (1, 3) else 1.0)
         table[j] = jnp.broadcast_to(column, (channels, width))
+
+
+def block_kernel(
+    flags, win, table, mid_alone, mid_both, mid_rest, out_alone, out_both, out_rest,
+    own_ref, previous_ref, oldest_ref, low_ref, high_ref, out_hbm, sum_ref,
+    out_ref, left, gathered, planes, act_one, act_two, h0_ref, total, stage, order, tiles_ref,
+):
+    rows, count = previous_ref.shape[0], previous_ref.shape[1]
+    channels, width = table.shape[1], table.shape[2]
+    pairs = width // 2
+    mid_parts = mid_alone, mid_both, mid_rest
+    out_parts = out_alone, out_both, out_rest
+    block = 3 * channels
+    begin = block // 256 * 256
+    end = 3 * block // 256 * 256 + 256
+    keep, keep_older, top, bottom = (flags[i : i + 1] for i in range(4))
     total[...] = jnp.zeros_like(total)
 
     span = 3 * pairs
@@ -109,11 +147,12 @@
     pick = jnp.where(pick, 1.0, 0.0).astype(BF16)
     sources = ((0, oldest_ref, 6, 2, 4), (2, previous_ref, 3, 0, 4), (6, own_ref, 0, 0, 2),
                (8, previous_ref, 3, 2, 4), (10, own_ref, 0, 0, 4))
-    for at, source, rim, begin, end in sources:
-        to = slice(at, at + end - begin)
-        gathered[3 : rows + 3, to] = source[:, begin:end].astype(F32)
-        gathered[:3, to] = low_ref[rim : rim + 3, begin:end].astype(F32)
-        gathered[rows + 3 :, to] = high_ref[rim : rim + 3, begin:end].astype(F32)
+    for at, source, rim, old, new in sources:
+        to = slice(at, at + new - old)
+        edge = 3 if source is own_ref else 0
+        gathered[3 : rows + 3, to] = source[edge : rows + edge, old:new].astype(F32)
+        gathered[:3, to] = low_ref[rim : rim + 3, old:new].astype(F32)
+        gathered[rows + 3 :, to] = high_ref[rim : rim + 3, old:new].astype(F32)
     gathered[:, 14:] = jnp.zeros((rows + 6, 2, 3 * width), F32)
     frames = (rows + 6) * 2 * SLOTS
     flat = gathered[...].reshape(frames, 3 * width).astype(BF16)
@@ -144,10 +183,26 @@
         inside = jnp.where(row < rim, top, 1.0)
         return inside * jnp.where(row >= extent - rim, bottom, 1.0)
 
-    def taps_of(source, row, t):
-        return jnp.concatenate(
-            [source[row + dr, t : t + 3].reshape(3 * channels, width) for dr in range(3)], axis=0
-        )
+    def pair_units(source, parts, row, frames, done):
+        alone, both, rest = parts
+
+        def start(t):
+            taps = jnp.concatenate(
+                [source[row + dr, t : t + 3].reshape(block, width) for dr in range(4)], axis=0
+            )
+            shared = jnp.dot(both[...], taps[begin:end], preferred_element_type=F32)
+            first = jnp.dot(alone[...], taps[:begin], preferred_element_type=F32)
+            second = jnp.dot(rest[...], taps[end:], preferred_element_type=F32)
+            return (shared[:block], first), (shared[block:], second)
+
+        def finish(dr, t, products):
+            one, other = products[dr]
+            done(dr, t, one + other)
+
+        return [
+            (functools.partial(start, t), [functools.partial(finish, dr, t) for dr in range(2)])
+            for t in range(frames)
+        ]
 
     def first_units(row):
         mask = row_mask(row, 2, rows + 4)
@@ -174,67 +229,67 @@
         ]
 
     def middle_units(row):
-        mask = row_mask(row, 1, rows + 2)
-
-        def start(t):
-            return jnp.dot(wmid[...], taps_of(act_one, row, t), preferred_element_type=F32)
-
-        def end(t, product):
+        def done(dr, t, product):
+            mask = row_mask(row + dr, 1, rows + 2)
             h1 = shifted_sum(product, channels) + table[2]
             act = rms_silu(h1, table[3], mask * keep if t < 2 else mask)
-            act_two[row, t] = act.astype(BF16)
-
-        return [
-            (functools.partial(start, t), [functools.partial(end, t)]) for t in range(count + 2)
-        ]
+            act_two[row + dr, t] = act.astype(BF16)
+
+        return pair_units(act_one, mid_parts, row, count + 2, done)
 
     def last_units(row):
-        def start(t):
-            return jnp.dot(wout[...], taps_of(act_two, row, t), preferred_element_type=F32)
-
-        def end(t, product):
+        def done(dr, t, product):
             value = shifted_sum(product, channels) + table[4]
-            value = (value + h0_ref[row + 2, t].astype(F32)).astype(BF16)
+            value = (value + h0_ref[row + dr + 2, t].astype(F32)).astype(BF16)
             total[...] += value.astype(F32)
-            stage[t, :channels] = value
-
-        return [(functools.partial(start, t), [functools.partial(end, t)]) for t in range(count)]
-
-    def written_units():
+            stage[dr, t, :channels] = value
+
+        return pair_units(act_two, out_parts, row, count, done)
+
+    def written_units(dr):
         lane = lax.broadcasted_iota(jnp.int32, (128, 128), 1)
 
-        def start(piece):
-            half = slice(piece // 2 * 128, piece // 2 * 128 + 128)
+        def turned_piece(half, odd):
             sides = []
             for t in range(0, count, 2):
-                one, two = stage[t, :, half].astype(F32), stage[t + 1, :, half].astype(F32)
-                if piece % 2:
+                one = stage[dr, t, :, half * 128 : half * 128 + 128].astype(F32)
+                two = stage[dr, t + 1, :, half * 128 : half * 128 + 128].astype(F32)
+                if odd:
                     one = pltpu.roll(one, part, 1)
                 else:
                     two = pltpu.roll(two, part, 1)
-                sides.append(jnp.where(lane < part, one, two).astype(BF16))
-            return lax.dot_general(
-                order[...], jnp.concatenate(sides, axis=1), (((1,), (1,)), ((), ())),
-                preferred_element_type=F32,
-            )
-
-        def end(piece, product):
-            pixels = [product[i * part : (i + 1) * part] for i in range(4)]
+                sides.append(jnp.transpose(jnp.where(lane < part, one, two)))
+            return jnp.concatenate(sides, axis=0).astype(BF16)
+
+        def start(half):
+            both = jnp.concatenate([turned_piece(half, odd) for odd in range(2)], axis=1)
+            return jnp.dot(order[...], both, preferred_element_type=F32)
+
+        def end(half, odd, product):
+            piece = 2 * half + odd
+            pixels = [
+                product[i * part : (i + 1) * part, odd * 128 : odd * 128 + 128] for i in range(4)
+            ]
             pixels = [pltpu.roll(x, 128 - 32 * i, 1) if i else x for i, x in enumerate(pixels)]
             lane = lax.broadcasted_iota(jnp.int32, (part, 128), 1)
             for j in range(3):
                 tile = jnp.where(lane < 96 - 32 * j, pixels[j], pixels[j + 1])
                 for group in range(part // count):
                     at = (3 * (piece * part // count + group) + j) * 128
-                    tiles_ref[:, at : at + 128] = tile[group * count : (group + 1) * count]
+                    tiles_ref[dr, :, at : at + 128] = tile[group * count : (group + 1) * count]
 
         return [
-            (functools.partial(start, piece), [functools.partial(end, piece)])
-            for piece in range(4)
+            (functools.partial(start, half), [functools.partial(end, half, odd) for odd in range(2)])
+            for half in range(2)
         ]
 
+    def sent(row):
+        pair = pl.ds(row, 2)
+        return pltpu.make_async_copy(out_ref.at[pair], out_hbm.at[pair], left.at[row // 2])
+
     def written(row):
-        out_ref[row] = tiles_ref[...].astype(BF16)
+        for dr in range(2):
+            out_ref[row + dr] = tiles_ref[dr].astype(BF16)
 
     def mixed(first, second):
         units = []
@@ -243,29 +298,40 @@
         return units
 
     def loop(begin, end, body):
-        def step(row, carry):
-            body(row)
+        def step(pair, carry):
+            body(pair * 2)
             return carry
 
         lax.fori_loop(begin, end, step, 0)
 
-    loop(0, 3, lambda row: pipelined(first_units(row)))
-    loop(0, 3, lambda row: pipelined(mixed(middle_units(row), first_units(row + 3))))
+    def inputs(row):
+        return first_units(row) + first_units(row + 1)
 
     def steady(row, middle=True, first=True):
-        units = mixed(written_units(), middle_units(row + 3) if middle else [])
-        units += mixed(last_units(row), first_units(row + 6) if first else [])
+        units = mixed(
+            written_units(0) + written_units(1), middle_units(row + 4) if middle else []
+        )
+        units += mixed(last_units(row), inputs(row + 8) if first else [])
         pipelined(units)
-        written(jnp.maximum(row - 1, 0))
-
-    loop(0, rows - 2, steady)
-    loop(rows - 2, rows - 1, lambda row: steady(row, first=False))
-    loop(rows - 1, rows, lambda row: steady(row, middle=False, first=False))
-    pipelined(written_units())
-    written(rows - 1)
-    clip = lax.broadcasted_iota(jnp.int32, sum_ref.shape, 1)
+        written(jnp.maximum(row - 2, 0))
+
+        @pl.when(row > 0)
+        def _():
+            sent(row - 2).start()
+
+    pairs = rows // 2
+    pipelined(inputs(0) + inputs(2))
+    loop(0, 2, lambda row: pipelined(mixed(middle_units(row), inputs(row + 4))))
+    loop(0, pairs - 2, steady)
+    loop(pairs - 2, pairs - 1, lambda row: steady(row, first=False))
+    loop(pairs - 1, pairs, lambda row: steady(row, middle=False, first=False))
+    pipelined(written_units(0) + written_units(1))
+    written(rows - 2)
+    sent(rows - 2).start()
     weighted = jnp.sum(total[...] * table[5], keepdims=True)
-    sum_ref[...] = jnp.where(clip == clip_id, jnp.broadcast_to(weighted, sum_ref.shape), 0.0)
+    sum_ref[...] = jnp.broadcast_to(weighted * flags[4:5, :128], sum_ref.shape)
+    for pair in range(pairs):
+        sent(2 * pair).wait()
 
 
 def local(
@@ -280,41 +346,56 @@
     own = frames.transpose(1, 0, 2)
     previous = moved(own, POSITION, 1)
     oldest = moved(own, POSITION, 2)
-    spans = (own, previous, oldest)
+    padded = lax.optimization_barrier(jnp.pad(own, ((3, 3), (0, 0), (0, 0))))
+    spans = (padded[3 : rows + 3], previous, oldest)
     low = moved(jnp.concatenate([x[rows - 3 :] for x in spans], axis=0), "band", 1)
     high = moved(jnp.concatenate([x[:3] for x in spans], axis=0), "band", -1)
 
     win = in_weight.transpose(2, 1, 0, 3).reshape(27, 3, channels).astype(F32)
     win = jnp.pad(win, ((0, 0), (0, SLOTS - 3), (0, 0)))
+    clip_row = jnp.pad(segments.astype(F32), (0, channels - segments.shape[0]))
     cols = jnp.stack(
-        [in_bias, gain_one, mid_bias, gain_two, out_bias, head_weight, in_bias, in_bias]
+        [in_bias, gain_one, mid_bias, gain_two, out_bias, head_weight, clip_row, in_bias]
     )
+    block = 3 * channels
+    begin, end = block // 256 * 256, 3 * block // 256 * 256 + 256
+    parts = [(block, begin), (2 * block, end - begin), (block, 4 * block - end)] * 2
     vmem = pl.BlockSpec(memory_space=pltpu.VMEM)
+    prepared = pl.pallas_call(
+        prepared_kernel,
+        in_specs=[vmem] * 4,
+        out_specs=[vmem] * 9,
+        out_shape=[
+            jax.ShapeDtypeStruct((8, width), F32),
+            jax.ShapeDtypeStruct((count * channels, 28 * SLOTS), BF16),
+            jax.ShapeDtypeStruct((6, channels, width), F32),
+        ] + [jax.ShapeDtypeStruct(shape, BF16) for shape in parts],
+        compiler_params=pltpu.CompilerParams(vmem_limit_bytes=12 << 20),
+        cost_estimate=pl.CostEstimate(flops=10**9, bytes_accessed=6 * 10**6, transcendentals=0),
+    )(win, mid_weight.swapaxes(0, 1), out_weight.swapaxes(0, 1), cols)
     features, weighted = pl.pallas_call(
         block_kernel,
-        in_specs=[pl.BlockSpec(memory_space=pltpu.SMEM)] + [vmem] * 9,
-        out_specs=[vmem, vmem],
+        in_specs=[vmem] * 14,
+        out_specs=[pl.BlockSpec(memory_space=pltpu.HBM), vmem],
         out_shape=[
             jax.ShapeDtypeStruct((rows, count, width * channels), BF16),
             jax.ShapeDtypeStruct((devices, 128), F32),
         ],
         scratch_shapes=[
+            pltpu.VMEM((rows, count, width * channels), BF16),
+            pltpu.SemaphoreType.DMA((rows // 2,)),
             pltpu.VMEM((rows + 6, 2 * SLOTS, 3 * width), F32),
             pltpu.VMEM((9, rows + 6, 2 * SLOTS, width), F32),
-            pltpu.VMEM((count * channels, 28 * SLOTS), BF16),
-            pltpu.VMEM((3 * channels, 9 * channels), BF16),
-            pltpu.VMEM((3 * channels, 9 * channels), BF16),
             pltpu.VMEM((rows + 4, count + 4, channels, width), BF16),
             pltpu.VMEM((rows + 2, count + 2, channels, width), BF16),
             pltpu.VMEM((rows + 4, count, channels, width), BF16),
-            pltpu.VMEM((6, channels, width), F32),
             pltpu.VMEM((channels, width), F32),
-            pltpu.VMEM((count, 128, width), BF16),
+            pltpu.VMEM((2, count, 128, width), BF16),
             pltpu.VMEM((width, width), BF16),
-            pltpu.VMEM((count, width * channels), F32),
+            pltpu.VMEM((2, count, width * channels), F32),
         ],
-        compiler_params=pltpu.CompilerParams(vmem_limit_bytes=56 << 20),
-    )(segments, own, previous, oldest, low, high, win, mid_weight, out_weight, cols)
+        compiler_params=pltpu.CompilerParams(vmem_limit_bytes=32 << 20),
+    )(*prepared, padded, previous, oldest, low, high)
     features = features.transpose(1, 0, 2)
 
     clips = targets.shape[0]

time: 72.7 us -> 70 us (0.963)
  starting transfers between devices: 17.8 us -> 16.2 us
    all_to_all x1, starting transfers between devices: 4.66 us -> 3.02 us  [local(): gathered = lax.all_to_all(weighted, EVERY, 0, 0, tiled=True)]
    transpose x0 -> x1, local copies, waits for them, and re-layouts: none -> 1.38 us  [local(): out_weight.swapaxes(0, 1)]
    another operation x1 -> x2, local copies, waits for them, and re-layouts: 1.37 us -> 0.03 us  [local(): jnp.stack([in_bias, gain_one, mid_bias, gain_two, out_bias, head_weight,...]
    pad x0 -> x1, local copies, waits for them, and re-layouts: none -> 0.93 us  [local(): padded = lax.optimization_barrier(jnp.pad(own, ((3, 3), (0, 0), (0, 0))))]
    slice x3, local copies, waits for them, and re-layouts: 0.82 us -> 0.05 us  [local(): high = moved(jnp.concatenate([x[:3] for x in spans], axis=0), 'band', -1)]
    pallas_call x1 -> x2, Pallas kernels: 35.8 us -> 35.1 us  [the longest x1 33.8 us: local(): pl.pallas_call(block_kernel, in_specs=[vmem] * 14, out_specs=[pl.BlockSpe...]
  transfers between devices with their start and end apart: 5 -> 5, of which waited for: 3 -> 2; matrix products, arithmetic and copies ran while one was open for 5% -> 6% of each run, Pallas kernels for 0% -> 2%
where the time goes in v3:
time: 70 us; the launch traced here: 69.6 us
  Pallas kernels  35.1 us (50%)
  starting transfers between devices  16.2 us (23%)
  waiting for transfers between devices  9.82 us (14%)
  between operations  3.31 us (5%)
  local copies, waits for them, and re-layouts  3.19 us (5%)
  other arithmetic  2.04 us (3%)
    pallas_call x1, Pallas kernels, local(): pl.pallas_call(block_kernel, in_specs=[vmem] * 14, out_specs=[pl.BlockSpe...  33.8 us
    ppermute x4, starting transfers between devices, moved(): return lax.ppermute(block, axis, route)  13.2 us
    all_to_all x1, waiting for transfers between devices, local(): gathered = lax.all_to_all(weighted, EVERY, 0, 0, tiled=True)  6.35 us
    ppermute x4, waiting for transfers between devices, moved(): return lax.ppermute(block, axis, route)  3.47 us
    all_to_all x1, starting transfers between devices, local(): gathered = lax.all_to_all(weighted, EVERY, 0, 0, tiled=True)  3.02 us
  transfers between devices with their start and end apart: 5, of which 2 were waited for; matrix products, arithmetic and copies ran while one was open for 6% of the time, Pallas kernels for 2%

profile of v3, /device:TPU:0, one launch (start us, length us, event | category | flops | bytes accessed | tf_op | source)
XLA Modules:
  0.0 69.6 jit_solution(11744934509223785347)
XLA Ops:
  0.6 0.0 copy-start
  0.6 0.0 copy-start.1
  0.7 0.0 copy-start.2
  0.7 0.0 copy-start.3
  0.7 0.0 copy-start.4
  0.7 0.0 copy-start.5
  0.7 5.0 %collective-permute-start = (bf16[12,4,768]{2,1,0:T(4,128)(2,1)}, bf16[12,4,768]{2,1,0:T(4,128)(2,1)S(1)}, u32[]{:S(2)}, u32[]{:S(2)}) collective-permute-start(bf16[12,4,768]{2,1,0:T(4,128)(2,1)} %bitcast.23), channel_id=1, source_target_pairs={{0,4},{4,8},{8,12},{12,16},{16,20},{20,24},{24,28},{1,5},{5,9},{9,... | collective-permute-start | bytes 221192 | tf_op jit(solution)/shard_map/ppermute | solution.py:20
  5.7 3.4 %collective-permute-start.1 = (bf16[12,4,768]{2,1,0:T(4,128)(2,1)}, bf16[12,4,768]{2,1,0:T(4,128)(2,1)S(1)}, u32[]{:S(2)}, u32[]{:S(2)}) collective-permute-start(bf16[12,4,768]{2,1,0:T(4,128)(2,1)} %bitcast.24), channel_id=1, source_target_pairs={{0,8},{4,12},{8,16},{12,20},{16,24},{20,28},{1,9},{5,13},{9,17},{1... | collective-permute-start | bytes 221192 | tf_op jit(solution)/shard_map/ppermute | solution.py:20
  9.1 0.9 %pad.17.own_ref = bf16[18,4,768]{2,1,0:T(4,128)(2,1)S(1)} pad(bf16[12,4,768]{2,1,0:T(4,128)(2,1)} %bitcast.25, bf16[]{:T(256)} %constant.8.clone.1), padding=3_3x0_0x0_0 | pad | bytes 184322 | tf_op jit(solution)/shard_map/jit(_pad)/pad | solution.py:349
  10.1 0.8 %copy.23 = bf16[9,3,3,96]{3,2,1,0:T(4,128)(2,1)S(1)} copy(bf16[9,3,3,96]{3,1,0,2:T(4,128)(2,1)} %bitcast.27) | data formatting | bytes 31104 | tf_op jit(solution)/shard_map/convert_element_type | solution.py:354
  10.8 0.7 convert_element_type.21
  11.5 1.4 %copy_bitcast_fusion = (bf16[3,3,288,96]{3,2,1,0:T(8,128)(2,1)S(1)}, bf16[3,3,288,96]{3,2,1,0:T(8,128)(2,1)S(1)}) fusion(bf16[3,3,288,96]{3,2,1,0:T(8,128)(2,1)} %param.22, bf16[3,3,288,96]{3,2,1,0:T(8,128)(2,1)} %param.19), kind=kLoop, calls=%fused_computation | loop fusion | bytes 1990656 | tf_op jit(solution)/shard_map/transpose | solution.py:375
  12.9 0.0 copy-done
  12.9 0.0 copy-done.1
  12.9 0.0 copy-done.2
  12.9 0.0 copy-done.3
  12.9 0.0 copy-done.4
  12.9 0.0 copy-done.5
  13.0 0.0 collective-permute-done.previous_ref
  13.0 0.0 collective-permute-done.1.oldest_ref
  13.1 3.5 %collective-permute-start.2 = (bf16[9,4,768]{2,1,0:T(4,128)(2,1)S(1)}, bf16[9,4,768]{2,1,0:T(4,128)(2,1)S(1)}, u32[]{:S(2)}, u32[]{:S(2)}) collective-permute-start(bf16[9,4,768]{2,1,0:T(4,128)(2,1)S(1)} %pad_maximum_fusion), channel_id=1, source_target_pairs={{0,1},{1,2},{2,3},{4,5},{5,6},{6,7},{8,9},{9,10},{10,11},{12,13},{... | collective-permute-start | bytes 165896 | tf_op jit(solution)/shard_map/ppermute | solution.py:20
  16.7 1.3 %collective-permute-start.3 = (bf16[9,4,768]{2,1,0:T(4,128)(2,1)S(1)}, bf16[9,4,768]{2,1,0:T(4,128)(2,1)S(1)}, u32[]{:S(2)}, u32[]{:S(2)}) collective-permute-start(bf16[9,4,768]{2,1,0:T(4,128)(2,1)S(1)} %pad_maximum_fusion.1), channel_id=1, source_target_pairs={{1,0},{2,1},{3,2},{5,4},{6,5},{7,6},{9,8},{10,9},{11,10},{13,12},{... | collective-permute-start | bytes 165896 | tf_op jit(solution)/shard_map/ppermute | solution.py:20
  18.0 1.2 %shard_map.148 = (f32[8,256]{1,0:T(8,128)S(1)}, bf16[384,224]{1,0:T(8,128)(2,1)S(1)}, f32[6,96,256]{2,1,0:T(8,128)S(1)}, bf16[288,256]{1,0:T(8,128)(2,1)S(1)}, b...) custom-call(f32[27,8,96]{2,1,0:T(8,128)S(1)} %pad_convert_fusion.win, ...), custom_call_target="tpu_custom_call" | custom-call | flops 1000000000 | bytes 6000000 | tf_op jit(solution)/shard_map/pallas_call | solution.py:364
  19.2 0.0 copy-start.7
  19.2 0.0 copy-start.6
  19.2 0.0 collective-permute-done.2.low_ref
  19.2 3.5 %collective-permute-done.3.high_ref = bf16[9,4,768]{2,1,0:T(4,128)(2,1)S(1)} collective-permute-done((bf16[9,4,768]{2,1,0:T(4,128)(2,1)S(1)}, bf16[9,4,768]{2,1,0:T(4,128)(2,1)S(1)}, u32[]{:S(2)}, u32[]{:S(2)}) %collective-permute-start.3) | collective-permute-done | bytes 55328 | tf_op jit(solution)/shard_map/ppermute | solution.py:20
  22.7 33.8 %shard_map.149 = (bf16[12,4,24576]{2,1,0:T(4,128)(2,1)}, f32[32,128]{1,0:T(8,128)}) custom-call(f32[8,256]{1,0:T(8,128)S(1)} %get-tuple-element.14.flags, bf16[384,224]{1,0:T(8,128)(2,1)S(1)} %get-tuple-element.15.win, f32[6,96,256]{2,1,0:T(8,128)S(1)} %get-tuple-element.16.table, bf16[288,256]{1,0:T(8,128)(2,1)S(1)} %get-tuple-element.17.mid_alone, ...), custom_call_target="tpu_custom_call" | custom-call | tf_op jit(solution)/shard_map/pallas_call | solution.py:376
  56.5 3.0 %all-to-all-start = ((f32[32,1,128]{2,1,0:T(1,128)}), f32[32,1,128]{2,1,0:T(1,128)S(1)}, u32[]{:S(2)}, u32[]{:S(2)}) async-start(f32[32,1,128]{2,1,0:T(1,128)} %bitcast.14), calls=%async_computation | async-start | bytes 32768 | tf_op jit(solution)/shard_map/all_to_all | solution.py:402
  59.5 0.0 copy-done.7
  59.6 0.1 convert_reduce_fusion
  60.3 6.3 %all-to-all-done = f32[32,1,128]{2,1,0:T(1,128)S(1)} async-done(((f32[32,1,128]{2,1,0:T(1,128)}), f32[32,1,128]{2,1,0:T(1,128)S(1)}, u32[]{:S(2)}, u32[]{:S(2)}) %all-to-all-start) | async-done | bytes 16416 | tf_op jit(solution)/shard_map/all_to_all | solution.py:402
  66.7 0.0 copy-done.6
  66.7 1.1 %multiply_reduce_fusion = (f32[]{:T(128)}, f32[4]{0:T(128)}) fusion(f32[4]{0:T(128)S(1)} %copy-done.6, f32[]{:T(128)} %bitcast.21, f32[4]{0:T(128)S(1)} %slice_reduce_fusion, f32[4]{0:T(128)S(1)} %convert_reduce_fusion), kind=kLoop, calls=%fused_computation.8 | loop fusion | flops 23 | bytes 72 | tf_op jit(solution)/shard_map/reduce_sum | solution.py:408
  (9 shorter events, 0.2 us)
Async XLA Ops:
  0.6 12.2 %copy-start = (f32[96]{0:T(128)S(1)}, f32[96]{0:T(128)}, u32[]{:S(2)}) copy-start(f32[96]{0:T(128)} %param.17) | copy-start | bytes 1156
  0.6 12.2 %copy-start.1 = (f32[96]{0:T(128)S(1)}, f32[96]{0:T(128)}, u32[]{:S(2)}) copy-start(f32[96]{0:T(128)} %param.18) | copy-start | bytes 1156
  0.7 12.2 %copy-start.2 = (f32[96]{0:T(128)S(1)}, f32[96]{0:T(128)}, u32[]{:S(2)}) copy-start(f32[96]{0:T(128)} %param.20) | copy-start | bytes 1156
  0.7 12.2 %copy-start.3 = (f32[96]{0:T(128)S(1)}, f32[96]{0:T(128)}, u32[]{:S(2)}) copy-start(f32[96]{0:T(128)} %param.21) | copy-start | bytes 1156
  0.7 12.2 %copy-start.4 = (f32[96]{0:T(128)S(1)}, f32[96]{0:T(128)}, u32[]{:S(2)}) copy-start(f32[96]{0:T(128)} %param.23) | copy-start | bytes 1156
  0.7 12.2 %copy-start.5 = (f32[96]{0:T(128)S(1)}, f32[96]{0:T(128)}, u32[]{:S(2)}) copy-start(f32[96]{0:T(128)} %param.24) | copy-start | bytes 1156
  0.7 12.3 %collective-permute-start = (bf16[12,4,768]{2,1,0:T(4,128)(2,1)}, bf16[12,4,768]{2,1,0:T(4,128)(2,1)S(1)}, u32[]{:S(2)}, u32[]{:S(2)}) collective-permute-start(bf16[12,4,768]{2,1,0:T(4,128)(2,1)} %bitcast.23), channel_id=1, source_target_pairs={{0,4},{4,8},{8,12},{12,16},{16,20},{20,24},{24,28},{1,5},{5,9},{9,... | collective-permute-start | bytes 221192 | tf_op jit(solution)/shard_map/ppermute | solution.py:20
  5.7 7.3 %collective-permute-start.1 = (bf16[12,4,768]{2,1,0:T(4,128)(2,1)}, bf16[12,4,768]{2,1,0:T(4,128)(2,1)S(1)}, u32[]{:S(2)}, u32[]{:S(2)}) collective-permute-start(bf16[12,4,768]{2,1,0:T(4,128)(2,1)} %bitcast.24), channel_id=1, source_target_pairs={{0,8},{4,12},{8,16},{12,20},{16,24},{20,28},{1,9},{5,13},{9,17},{1... | collective-permute-start | bytes 221192 | tf_op jit(solution)/shard_map/ppermute | solution.py:20
  13.1 6.1 %collective-permute-start.2 = (bf16[9,4,768]{2,1,0:T(4,128)(2,1)S(1)}, bf16[9,4,768]{2,1,0:T(4,128)(2,1)S(1)}, u32[]{:S(2)}, u32[]{:S(2)}) collective-permute-start(bf16[9,4,768]{2,1,0:T(4,128)(2,1)S(1)} %pad_maximum_fusion), channel_id=1, source_target_pairs={{0,1},{1,2},{2,3},{4,5},{5,6},{6,7},{8,9},{9,10},{10,11},{12,13},{... | collective-permute-start | bytes 165896 | tf_op jit(solution)/shard_map/ppermute | solution.py:20
  16.7 6.0 %collective-permute-start.3 = (bf16[9,4,768]{2,1,0:T(4,128)(2,1)S(1)}, bf16[9,4,768]{2,1,0:T(4,128)(2,1)S(1)}, u32[]{:S(2)}, u32[]{:S(2)}) collective-permute-start(bf16[9,4,768]{2,1,0:T(4,128)(2,1)S(1)} %pad_maximum_fusion.1), channel_id=1, source_target_pairs={{1,0},{2,1},{3,2},{5,4},{6,5},{7,6},{9,8},{10,9},{11,10},{13,12},{... | collective-permute-start | bytes 165896 | tf_op jit(solution)/shard_map/ppermute | solution.py:20
  19.2 40.3 %copy-start.7 = (s32[8]{0:T(128)S(1)}, s32[8]{0:T(128)}, u32[]{:S(2)}) copy-start(s32[8]{0:T(128)} %param.14) | copy-start | bytes 100
  19.2 47.5 %copy-start.6 = (f32[4]{0:T(128)S(1)}, f32[4]{0:T(128)}, u32[]{:S(2)}) copy-start(f32[4]{0:T(128)} %param.15) | copy-start | bytes 52
  56.5 10.2 %all-to-all-start = ((f32[32,1,128]{2,1,0:T(1,128)}), f32[32,1,128]{2,1,0:T(1,128)S(1)}, u32[]{:S(2)}, u32[]{:S(2)}) async-start(f32[32,1,128]{2,1,0:T(1,128)} %bitcast.14), calls=%async_computation | async-start | bytes 32768 | tf_op jit(solution)/shard_map/all_to_all | solution.py:402

commit v4 on v3

--- a/solution.py
+++ b/solution.py
@@ -298,25 +298,21 @@
         return units
 
     def loop(begin, end, body):
-        def step(pair, carry):
+        for pair in range(begin, end):
             body(pair * 2)
-            return carry
-
-        lax.fori_loop(begin, end, step, 0)
 
     def inputs(row):
         return first_units(row) + first_units(row + 1)
 
     def steady(row, middle=True, first=True):
         units = mixed(
-            written_units(0) + written_units(1), middle_units(row + 4) if middle else []
+            written_units(0) + written_units(1) if row else [],
+            middle_units(row + 4) if middle else [],
         )
         units += mixed(last_units(row), inputs(row + 8) if first else [])
         pipelined(units)
-        written(jnp.maximum(row - 2, 0))
-
-        @pl.when(row > 0)
-        def _():
+        if row:
+            written(row - 2)
             sent(row - 2).start()
 
     pairs = rows // 2

time: 70 us -> 67.7 us (0.967)
  Pallas kernels: 35.1 us -> 32.8 us
    pallas_call x1, Pallas kernels: 33.8 us -> 31.6 us  [local(): pl.pallas_call(block_kernel, in_specs=[vmem] * 14, out_specs=[pl.BlockSpe...]
where the time goes in v4:
time: 67.7 us; the launch traced here: 67.4 us
  Pallas kernels  32.8 us (48%)
  starting transfers between devices  16.2 us (24%)
  waiting for transfers between devices  9.82 us (15%)
  between operations  3.31 us (5%)
  local copies, waits for them, and re-layouts  3.19 us (5%)
  other arithmetic  2.04 us (3%)
    pallas_call x1, Pallas kernels, local(): pl.pallas_call(block_kernel, in_specs=[vmem] * 14, out_specs=[pl.BlockSpe...  31.6 us
    ppermute x4, starting transfers between devices, moved(): return lax.ppermute(block, axis, route)  13.2 us
    all_to_all x1, waiting for transfers between devices, local(): gathered = lax.all_to_all(weighted, EVERY, 0, 0, tiled=True)  6.35 us
    ppermute x4, waiting for transfers between devices, moved(): return lax.ppermute(block, axis, route)  3.47 us
    all_to_all x1, starting transfers between devices, local(): gathered = lax.all_to_all(weighted, EVERY, 0, 0, tiled=True)  3.01 us
    transpose x1, local copies, waits for them, and re-layouts, local(): out_weight.swapaxes(0, 1)  1.38 us
  transfers between devices with their start and end apart: 5, of which 2 were waited for; matrix products, arithmetic and copies ran while one was open for 6% of the time, Pallas kernels for 2%

profile of v4, /device:TPU:0, one launch (start us, length us, event | category | flops | bytes accessed | tf_op | source)
XLA Modules:
  0.0 67.4 jit_solution(10641473581286132651)
XLA Ops:
  0.6 0.0 copy-start
  0.6 0.0 copy-start.1
  0.7 0.0 copy-start.2
  0.7 0.0 copy-start.3
  0.7 0.0 copy-start.4
  0.7 0.0 copy-start.5
  0.7 5.0 %collective-permute-start = (bf16[12,4,768]{2,1,0:T(4,128)(2,1)}, bf16[12,4,768]{2,1,0:T(4,128)(2,1)S(1)}, u32[]{:S(2)}, u32[]{:S(2)}) collective-permute-start(bf16[12,4,768]{2,1,0:T(4,128)(2,1)} %bitcast.23), channel_id=1, source_target_pairs={{0,4},{4,8},{8,12},{12,16},{16,20},{20,24},{24,28},{1,5},{5,9},{9,... | collective-permute-start | bytes 221192 | tf_op jit(solution)/shard_map/ppermute | solution.py:20
  5.7 3.4 %collective-permute-start.1 = (bf16[12,4,768]{2,1,0:T(4,128)(2,1)}, bf16[12,4,768]{2,1,0:T(4,128)(2,1)S(1)}, u32[]{:S(2)}, u32[]{:S(2)}) collective-permute-start(bf16[12,4,768]{2,1,0:T(4,128)(2,1)} %bitcast.24), channel_id=1, source_target_pairs={{0,8},{4,12},{8,16},{12,20},{16,24},{20,28},{1,9},{5,13},{9,17},{1... | collective-permute-start | bytes 221192 | tf_op jit(solution)/shard_map/ppermute | solution.py:20
  9.1 0.9 %pad.17.own_ref = bf16[18,4,768]{2,1,0:T(4,128)(2,1)S(1)} pad(bf16[12,4,768]{2,1,0:T(4,128)(2,1)} %bitcast.25, bf16[]{:T(256)} %constant.8.clone.1), padding=3_3x0_0x0_0 | pad | bytes 184322 | tf_op jit(solution)/shard_map/jit(_pad)/pad | solution.py:345
  10.1 0.8 %copy.23 = bf16[9,3,3,96]{3,2,1,0:T(4,128)(2,1)S(1)} copy(bf16[9,3,3,96]{3,1,0,2:T(4,128)(2,1)} %bitcast.27) | data formatting | bytes 31104 | tf_op jit(solution)/shard_map/convert_element_type | solution.py:350
  10.8 0.7 convert_element_type.21
  11.5 1.4 %copy_bitcast_fusion = (bf16[3,3,288,96]{3,2,1,0:T(8,128)(2,1)S(1)}, bf16[3,3,288,96]{3,2,1,0:T(8,128)(2,1)S(1)}) fusion(bf16[3,3,288,96]{3,2,1,0:T(8,128)(2,1)} %param.22, bf16[3,3,288,96]{3,2,1,0:T(8,128)(2,1)} %param.19), kind=kLoop, calls=%fused_computation | loop fusion | bytes 1990656 | tf_op jit(solution)/shard_map/transpose | solution.py:371
  12.9 0.0 copy-done
  12.9 0.0 copy-done.1
  12.9 0.0 copy-done.2
  12.9 0.0 copy-done.3
  12.9 0.0 copy-done.4
  12.9 0.0 copy-done.5
  13.0 0.0 collective-permute-done.previous_ref
  13.0 0.0 collective-permute-done.1.oldest_ref
  13.1 3.5 %collective-permute-start.2 = (bf16[9,4,768]{2,1,0:T(4,128)(2,1)S(1)}, bf16[9,4,768]{2,1,0:T(4,128)(2,1)S(1)}, u32[]{:S(2)}, u32[]{:S(2)}) collective-permute-start(bf16[9,4,768]{2,1,0:T(4,128)(2,1)S(1)} %pad_maximum_fusion), channel_id=1, source_target_pairs={{0,1},{1,2},{2,3},{4,5},{5,6},{6,7},{8,9},{9,10},{10,11},{12,13},{... | collective-permute-start | bytes 165896 | tf_op jit(solution)/shard_map/ppermute | solution.py:20
  16.7 1.3 %collective-permute-start.3 = (bf16[9,4,768]{2,1,0:T(4,128)(2,1)S(1)}, bf16[9,4,768]{2,1,0:T(4,128)(2,1)S(1)}, u32[]{:S(2)}, u32[]{:S(2)}) collective-permute-start(bf16[9,4,768]{2,1,0:T(4,128)(2,1)S(1)} %pad_maximum_fusion.1), channel_id=1, source_target_pairs={{1,0},{2,1},{3,2},{5,4},{6,5},{7,6},{9,8},{10,9},{11,10},{13,12},{... | collective-permute-start | bytes 165896 | tf_op jit(solution)/shard_map/ppermute | solution.py:20
  18.0 1.2 %shard_map.148 = (f32[8,256]{1,0:T(8,128)S(1)}, bf16[384,224]{1,0:T(8,128)(2,1)S(1)}, f32[6,96,256]{2,1,0:T(8,128)S(1)}, bf16[288,256]{1,0:T(8,128)(2,1)S(1)}, b...) custom-call(f32[27,8,96]{2,1,0:T(8,128)S(1)} %pad_convert_fusion.win, ...), custom_call_target="tpu_custom_call" | custom-call | flops 1000000000 | bytes 6000000 | tf_op jit(solution)/shard_map/pallas_call | solution.py:360
  19.2 0.0 copy-start.7
  19.2 0.0 copy-start.6
  19.2 0.0 collective-permute-done.2.low_ref
  19.2 3.5 %collective-permute-done.3.high_ref = bf16[9,4,768]{2,1,0:T(4,128)(2,1)S(1)} collective-permute-done((bf16[9,4,768]{2,1,0:T(4,128)(2,1)S(1)}, bf16[9,4,768]{2,1,0:T(4,128)(2,1)S(1)}, u32[]{:S(2)}, u32[]{:S(2)}) %collective-permute-start.3) | collective-permute-done | bytes 55328 | tf_op jit(solution)/shard_map/ppermute | solution.py:20
  22.7 31.6 %shard_map.149 = (bf16[12,4,24576]{2,1,0:T(4,128)(2,1)}, f32[32,128]{1,0:T(8,128)}) custom-call(f32[8,256]{1,0:T(8,128)S(1)} %get-tuple-element.14.flags, bf16[384,224]{1,0:T(8,128)(2,1)S(1)} %get-tuple-element.15.win, f32[6,96,256]{2,1,0:T(8,128)S(1)} %get-tuple-element.16.table, bf16[288,256]{1,0:T(8,128)(2,1)S(1)} %get-tuple-element.17.mid_alone, ...), custom_call_target="tpu_custom_call" | custom-call | tf_op jit(solution)/shard_map/pallas_call | solution.py:372
  54.3 3.0 %all-to-all-start = ((f32[32,1,128]{2,1,0:T(1,128)}), f32[32,1,128]{2,1,0:T(1,128)S(1)}, u32[]{:S(2)}, u32[]{:S(2)}) async-start(f32[32,1,128]{2,1,0:T(1,128)} %bitcast.14), calls=%async_computation | async-start | bytes 32768 | tf_op jit(solution)/shard_map/all_to_all | solution.py:398
  57.3 0.0 copy-done.7
  57.3 0.1 convert_reduce_fusion
  58.1 6.3 %all-to-all-done = f32[32,1,128]{2,1,0:T(1,128)S(1)} async-done(((f32[32,1,128]{2,1,0:T(1,128)}), f32[32,1,128]{2,1,0:T(1,128)S(1)}, u32[]{:S(2)}, u32[]{:S(2)}) %all-to-all-start) | async-done | bytes 16416 | tf_op jit(solution)/shard_map/all_to_all | solution.py:398
  64.4 0.0 copy-done.6
  64.5 1.1 %multiply_reduce_fusion = (f32[]{:T(128)}, f32[4]{0:T(128)}) fusion(f32[4]{0:T(128)S(1)} %copy-done.6, f32[]{:T(128)} %bitcast.21, f32[4]{0:T(128)S(1)} %slice_reduce_fusion, f32[4]{0:T(128)S(1)} %convert_reduce_fusion), kind=kLoop, calls=%fused_computation.8 | loop fusion | flops 23 | bytes 72 | tf_op jit(solution)/shard_map/reduce_sum | solution.py:404
  (9 shorter events, 0.2 us)
Async XLA Ops:
  0.6 12.2 %copy-start = (f32[96]{0:T(128)S(1)}, f32[96]{0:T(128)}, u32[]{:S(2)}) copy-start(f32[96]{0:T(128)} %param.17) | copy-start | bytes 1156
  0.6 12.2 %copy-start.1 = (f32[96]{0:T(128)S(1)}, f32[96]{0:T(128)}, u32[]{:S(2)}) copy-start(f32[96]{0:T(128)} %param.18) | copy-start | bytes 1156
  0.7 12.2 %copy-start.2 = (f32[96]{0:T(128)S(1)}, f32[96]{0:T(128)}, u32[]{:S(2)}) copy-start(f32[96]{0:T(128)} %param.20) | copy-start | bytes 1156
  0.7 12.2 %copy-start.3 = (f32[96]{0:T(128)S(1)}, f32[96]{0:T(128)}, u32[]{:S(2)}) copy-start(f32[96]{0:T(128)} %param.21) | copy-start | bytes 1156
  0.7 12.2 %copy-start.4 = (f32[96]{0:T(128)S(1)}, f32[96]{0:T(128)}, u32[]{:S(2)}) copy-start(f32[96]{0:T(128)} %param.23) | copy-start | bytes 1156
  0.7 12.2 %copy-start.5 = (f32[96]{0:T(128)S(1)}, f32[96]{0:T(128)}, u32[]{:S(2)}) copy-start(f32[96]{0:T(128)} %param.24) | copy-start | bytes 1156
  0.7 12.3 %collective-permute-start = (bf16[12,4,768]{2,1,0:T(4,128)(2,1)}, bf16[12,4,768]{2,1,0:T(4,128)(2,1)S(1)}, u32[]{:S(2)}, u32[]{:S(2)}) collective-permute-start(bf16[12,4,768]{2,1,0:T(4,128)(2,1)} %bitcast.23), channel_id=1, source_target_pairs={{0,4},{4,8},{8,12},{12,16},{16,20},{20,24},{24,28},{1,5},{5,9},{9,... | collective-permute-start | bytes 221192 | tf_op jit(solution)/shard_map/ppermute | solution.py:20
  5.7 7.3 %collective-permute-start.1 = (bf16[12,4,768]{2,1,0:T(4,128)(2,1)}, bf16[12,4,768]{2,1,0:T(4,128)(2,1)S(1)}, u32[]{:S(2)}, u32[]{:S(2)}) collective-permute-start(bf16[12,4,768]{2,1,0:T(4,128)(2,1)} %bitcast.24), channel_id=1, source_target_pairs={{0,8},{4,12},{8,16},{12,20},{16,24},{20,28},{1,9},{5,13},{9,17},{1... | collective-permute-start | bytes 221192 | tf_op jit(solution)/shard_map/ppermute | solution.py:20
  13.1 6.1 %collective-permute-start.2 = (bf16[9,4,768]{2,1,0:T(4,128)(2,1)S(1)}, bf16[9,4,768]{2,1,0:T(4,128)(2,1)S(1)}, u32[]{:S(2)}, u32[]{:S(2)}) collective-permute-start(bf16[9,4,768]{2,1,0:T(4,128)(2,1)S(1)} %pad_maximum_fusion), channel_id=1, source_target_pairs={{0,1},{1,2},{2,3},{4,5},{5,6},{6,7},{8,9},{9,10},{10,11},{12,13},{... | collective-permute-start | bytes 165896 | tf_op jit(solution)/shard_map/ppermute | solution.py:20
  16.7 6.0 %collective-permute-start.3 = (bf16[9,4,768]{2,1,0:T(4,128)(2,1)S(1)}, bf16[9,4,768]{2,1,0:T(4,128)(2,1)S(1)}, u32[]{:S(2)}, u32[]{:S(2)}) collective-permute-start(bf16[9,4,768]{2,1,0:T(4,128)(2,1)S(1)} %pad_maximum_fusion.1), channel_id=1, source_target_pairs={{1,0},{2,1},{3,2},{5,4},{6,5},{7,6},{9,8},{10,9},{11,10},{13,12},{... | collective-permute-start | bytes 165896 | tf_op jit(solution)/shard_map/ppermute | solution.py:20
  19.2 38.1 %copy-start.7 = (s32[8]{0:T(128)S(1)}, s32[8]{0:T(128)}, u32[]{:S(2)}) copy-start(s32[8]{0:T(128)} %param.14) | copy-start | bytes 100
  19.2 45.2 %copy-start.6 = (f32[4]{0:T(128)S(1)}, f32[4]{0:T(128)}, u32[]{:S(2)}) copy-start(f32[4]{0:T(128)} %param.15) | copy-start | bytes 52
  54.3 10.1 %all-to-all-start = ((f32[32,1,128]{2,1,0:T(1,128)}), f32[32,1,128]{2,1,0:T(1,128)S(1)}, u32[]{:S(2)}, u32[]{:S(2)}) async-start(f32[32,1,128]{2,1,0:T(1,128)} %bitcast.14), calls=%async_computation | async-start | bytes 32768 | tf_op jit(solution)/shard_map/all_to_all | solution.py:398

commit v5 on v4

--- a/solution.py
+++ b/solution.py
@@ -11,6 +11,7 @@
 F32 = jnp.float32
 POSITION = ("clip", "span")
 EVERY = ("clip", "span", "band")
+HANDED = 160
 SLOTS = 8
 
 
@@ -52,9 +53,17 @@
         end()
 
 
+def split_three(row, channels):
+    high = row.astype(BF16).astype(F32)
+    middle = (row - high).astype(BF16).astype(F32)
+    low = row - high - middle
+    rows = jnp.concatenate([high, middle, low, jnp.zeros((5, channels), F32)], axis=0)
+    return rows.astype(BF16)
+
+
 def prepared_kernel(
     win_ref, wmid_ref, wout_ref, cols_ref,
-    flags, win, table, mid_alone, mid_both, mid_rest, out_alone, out_both, out_rest,
+    flags, win, table, coefs, mid_alone, mid_both, mid_rest, out_alone, out_both, out_rest,
 ):
     width, channels = table.shape[2], cols_ref.shape[1]
     count = win.shape[0] // channels
@@ -92,6 +101,7 @@
     block = 3 * channels
     begin = block // 256 * 256
     end = 3 * block // 256 * 256 + 256
+    head = split_three(cols_ref[5:6], channels)
     for source, (alone, both, rest) in ((wmid_ref, mid_parts), (wout_ref, out_parts)):
         for k in range(3):
             piece = jnp.concatenate(
@@ -101,6 +111,12 @@
                 ],
                 axis=0,
             )
+            if source is wout_ref:
+                toward = lax.dot_general(
+                    piece, head, (((1,), (1,)), ((), ())), preferred_element_type=F32
+                )
+                toward = jnp.sum(toward, axis=1, keepdims=True)
+                coefs[k] = jnp.broadcast_to(toward, (3 * block, 128))
             at = slice(k * channels, (k + 1) * channels)
             beside = slice(block + k * channels, block + (k + 1) * channels)
             none = jnp.zeros((end - 3 * block, channels), BF16)
@@ -110,11 +126,7 @@
             both[beside] = turned(jnp.concatenate([none, piece[: end - block]], axis=0))
             rest[at] = turned(piece[end - block :])
 
-    bias = cols_ref[:1]
-    high = bias.astype(BF16).astype(F32)
-    middle = (bias - high).astype(BF16).astype(F32)
-    low = bias - high - middle
-    bias = jnp.concatenate([high, middle, low, jnp.zeros((5, channels), F32)], axis=0)
+    bias = split_three(cols_ref[:1], channels).astype(F32)
     for t in range(count):
         piece = pltpu.roll(win_ref[...], t, 1) if t else win_ref[...]
         piece = jnp.concatenate([piece.reshape(27 * SLOTS, channels), bias], axis=0)
@@ -125,10 +137,115 @@
         table[j] = jnp.broadcast_to(column, (channels, width))
 
 
+def order_of_pixels(order, stage, width, count):
+    part = width // 4
+    row = lax.broadcasted_iota(jnp.int32, (width, width), 0)
+    pixel = row % part // count * 4 + row // part
+    wanted = row % count * part + pixel
+    hit = lax.broadcasted_iota(jnp.int32, (width, width), 1) == wanted
+    order[...] = jnp.where(hit, 1.0, 0.0).astype(BF16)
+    stage[...] = jnp.zeros_like(stage)
+
+
+def pair_units(source, parts, row, frames, done):
+    channels, width = source.shape[2], source.shape[3]
+    block = 3 * channels
+    begin = block // 256 * 256
+    end = 3 * block // 256 * 256 + 256
+    alone, both, rest = parts
+
+    def start(t):
+        taps = jnp.concatenate(
+            [source[row + dr, t : t + 3].reshape(block, width) for dr in range(4)], axis=0
+        )
+        shared = jnp.dot(both[...], taps[begin:end], preferred_element_type=F32)
+        first = jnp.dot(alone[...], taps[:begin], preferred_element_type=F32)
+        second = jnp.dot(rest[...], taps[end:], preferred_element_type=F32)
+        return (shared[:block], first), (shared[block:], second)
+
+    def finish(dr, t, products):
+        one, other = products[dr]
+        done(dr, t, one + other)
+
+    return [
+        (functools.partial(start, t), [functools.partial(finish, dr, t) for dr in range(2)])
+        for t in range(frames)
+    ]
+
+
+def mixed(first, second):
+    units = []
+    for i in range(max(len(first), len(second))):
+        units += first[i : i + 1] + second[i : i + 1]
+    return units
+
+
+def writer(
+    act_two, h0_ref, lag, out_parts, table, stage, order, tiles_ref, out_ref, out_hbm, left, shift
+):
+    channels, width = act_two.shape[2], act_two.shape[3]
+    count, part = out_ref.shape[1], width // 4
+
+    def last_units(row):
+        def done(dr, t, product):
+            value = shifted_sum(product, channels) + table[4]
+            value = (value + h0_ref[row + dr + lag, t].astype(F32)).astype(BF16)
+            stage[dr, t, :channels] = value
+
+        return pair_units(act_two, out_parts, row, count, done)
+
+    def written_units(dr):
+        lane = lax.broadcasted_iota(jnp.int32, (128, 128), 1)
+
+        def turned_piece(half, odd):
+            sides = []
+            for t in range(0, count, 2):
+                one = stage[dr, t, :, half * 128 : half * 128 + 128].astype(F32)
+                two = stage[dr, t + 1, :, half * 128 : half * 128 + 128].astype(F32)
+                if odd:
+                    one = pltpu.roll(one, part, 1)
+                else:
+                    two = pltpu.roll(two, part, 1)
+                sides.append(jnp.transpose(jnp.where(lane < part, one, two)))
+            return jnp.concatenate(sides, axis=0).astype(BF16)
+
+        def start(half):
+            both = jnp.concatenate([turned_piece(half, odd) for odd in range(2)], axis=1)
+            return jnp.dot(order[...], both, preferred_element_type=F32)
+
+        def end(half, odd, product):
+            piece = 2 * half + odd
+            pixels = [
+                product[i * part : (i + 1) * part, odd * 128 : odd * 128 + 128] for i in range(4)
+            ]
+            pixels = [pltpu.roll(x, 128 - 32 * i, 1) if i else x for i, x in enumerate(pixels)]
+            lane = lax.broadcasted_iota(jnp.int32, (part, 128), 1)
+            for j in range(3):
+                tile = jnp.where(lane < 96 - 32 * j, pixels[j], pixels[j + 1])
+                for group in range(part // count):
+                    at = (3 * (piece * part // count + group) + j) * 128
+                    tiles_ref[dr, :, at : at + 128] = tile[group * count : (group + 1) * count]
+
+        return [
+            (functools.partial(start, half), [functools.partial(end, half, odd) for odd in range(2)])
+            for half in range(2)
+        ]
+
+    def sent(row):
+        here, there = pl.ds(row, 2), pl.ds(row + shift, 2)
+        return pltpu.make_async_copy(out_ref.at[here], out_hbm.at[there], left.at[row // 2])
+
+    def written(row):
+        for dr in range(2):
+            out_ref[row + dr] = tiles_ref[dr].astype(BF16)
+
+    return last_units, written_units, written, sent
+
+
 def block_kernel(
-    flags, win, table, mid_alone, mid_both, mid_rest, out_alone, out_both, out_rest,
-    own_ref, previous_ref, oldest_ref, low_ref, high_ref, out_hbm, sum_ref,
-    out_ref, left, gathered, planes, act_one, act_two, h0_ref, total, stage, order, tiles_ref,
+    flags, win, table, coefs, mid_alone, mid_both, mid_rest, out_alone, out_both, out_rest,
+    own_ref, previous_ref, oldest_ref, low_ref, high_ref, out_hbm, sum_ref, rest_hbm,
+    rest, handed, out_ref, left, gathered, planes, act_one, act_two, h0_ref, total, sums, stage, order, tiles_ref,
 ):
     rows, count = previous_ref.shape[0], previous_ref.shape[1]
     channels, width = table.shape[1], table.shape[2]
@@ -138,6 +255,13 @@
     block = 3 * channels
     begin = block // 256 * 256
     end = 3 * block // 256 * 256 + 256
+    early = out_ref.shape[0]
+    late = rows - early
+
+    def handing(row):
+        pair = pl.ds(row, 2), pl.ds(0, count if row >= late + 2 else count + 2)
+        return pltpu.make_async_copy(rest.at[pair], rest_hbm.at[pair], handed.at[row // 2])
+
     keep, keep_older, top, bottom = (flags[i : i + 1] for i in range(4))
     total[...] = jnp.zeros_like(total)
 
@@ -171,46 +295,24 @@
         plane = jnp.where(pixel == width - 1, 0.0, pltpu.roll(plane, width - 1, 1))
         planes[6 + c] = plane.reshape(planes.shape[1:])
 
-    part = width // 4
-    row = lax.broadcasted_iota(jnp.int32, (width, width), 0)
-    pixel = row % part // count * 4 + row // part
-    wanted = row % count * part + pixel
-    hit = lax.broadcasted_iota(jnp.int32, (width, width), 1) == wanted
-    order[...] = jnp.where(hit, 1.0, 0.0).astype(BF16)
-    stage[...] = jnp.zeros_like(stage)
+    order_of_pixels(order, stage, width, count)
+    sums[...] = jnp.zeros_like(sums)
 
     def row_mask(row, rim, extent):
         inside = jnp.where(row < rim, top, 1.0)
         return inside * jnp.where(row >= extent - rim, bottom, 1.0)
 
-    def pair_units(source, parts, row, frames, done):
-        alone, both, rest = parts
-
-        def start(t):
-            taps = jnp.concatenate(
-                [source[row + dr, t : t + 3].reshape(block, width) for dr in range(4)], axis=0
-            )
-            shared = jnp.dot(both[...], taps[begin:end], preferred_element_type=F32)
-            first = jnp.dot(alone[...], taps[:begin], preferred_element_type=F32)
-            second = jnp.dot(rest[...], taps[end:], preferred_element_type=F32)
-            return (shared[:block], first), (shared[block:], second)
-
-        def finish(dr, t, products):
-            one, other = products[dr]
-            done(dr, t, one + other)
-
-        return [
-            (functools.partial(start, t), [functools.partial(finish, dr, t) for dr in range(2)])
-            for t in range(frames)
-        ]
-
     def first_units(row):
         mask = row_mask(row, 2, rows + 4)
 
         def end(t, at, product):
             h0 = product[at : at + channels].astype(BF16)
-            if t >= 4:
-                h0_ref[row, t - 4] = h0
+            if t >= 4 and 2 <= row < rows + 2:
+                total[...] += h0.astype(F32)
+                if row < early + 2:
+                    h0_ref[row, t - 4] = h0
+                else:
+                    rest[late + row - early, t - 4] = h0
             act = rms_silu(h0.astype(F32), table[1], mask * keep if t < 4 else mask)
             act_one[row, t] = act.astype(BF16)
 
@@ -233,69 +335,16 @@
             mask = row_mask(row + dr, 1, rows + 2)
             h1 = shifted_sum(product, channels) + table[2]
             act = rms_silu(h1, table[3], mask * keep if t < 2 else mask)
-            act_two[row + dr, t] = act.astype(BF16)
+            if row + dr < early + 2:
+                act_two[row + dr, t] = act.astype(BF16)
+            if row + dr >= early:
+                rest[row + dr - early, t] = act.astype(BF16)
+            kind = min(row + dr, 2) + max(row + dr - rows + 1, 0)
+            for later in range(3):
+                if 0 <= t - later < count:
+                    sums[5 * later + kind] += act
 
         return pair_units(act_one, mid_parts, row, count + 2, done)
-
-    def last_units(row):
-        def done(dr, t, product):
-            value = shifted_sum(product, channels) + table[4]
-            value = (value + h0_ref[row + dr + 2, t].astype(F32)).astype(BF16)
-            total[...] += value.astype(F32)
-            stage[dr, t, :channels] = value
-
-        return pair_units(act_two, out_parts, row, count, done)
-
-    def written_units(dr):
-        lane = lax.broadcasted_iota(jnp.int32, (128, 128), 1)
-
-        def turned_piece(half, odd):
-            sides = []
-            for t in range(0, count, 2):
-                one = stage[dr, t, :, half * 128 : half * 128 + 128].astype(F32)
-                two = stage[dr, t + 1, :, half * 128 : half * 128 + 128].astype(F32)
-                if odd:
-                    one = pltpu.roll(one, part, 1)
-                else:
-                    two = pltpu.roll(two, part, 1)
-                sides.append(jnp.transpose(jnp.where(lane < part, one, two)))
-            return jnp.concatenate(sides, axis=0).astype(BF16)
-
-        def start(half):
-            both = jnp.concatenate([turned_piece(half, odd) for odd in range(2)], axis=1)
-            return jnp.dot(order[...], both, preferred_element_type=F32)
-
-        def end(half, odd, product):
-            piece = 2 * half + odd
-            pixels = [
-                product[i * part : (i + 1) * part, odd * 128 : odd * 128 + 128] for i in range(4)
-            ]
-            pixels = [pltpu.roll(x, 128 - 32 * i, 1) if i else x for i, x in enumerate(pixels)]
-            lane = lax.broadcasted_iota(jnp.int32, (part, 128), 1)
-            for j in range(3):
-                tile = jnp.where(lane < 96 - 32 * j, pixels[j], pixels[j + 1])
-                for group in range(part // count):
-                    at = (3 * (piece * part // count + group) + j) * 128
-                    tiles_ref[dr, :, at : at + 128] = tile[group * count : (group + 1) * count]
-
-        return [
-            (functools.partial(start, half), [functools.partial(end, half, odd) for odd in range(2)])
-            for half in range(2)
-        ]
-
-    def sent(row):
-        pair = pl.ds(row, 2)
-        return pltpu.make_async_copy(out_ref.at[pair], out_hbm.at[pair], left.at[row // 2])
-
-    def written(row):
-        for dr in range(2):
-            out_ref[row + dr] = tiles_ref[dr].astype(BF16)
-
-    def mixed(first, second):
-        units = []
-        for i in range(max(len(first), len(second))):
-            units += first[i : i + 1] + second[i : i + 1]
-        return units
 
     def loop(begin, end, body):
         for pair in range(begin, end):
@@ -304,30 +353,84 @@
     def inputs(row):
         return first_units(row) + first_units(row + 1)
 
-    def steady(row, middle=True, first=True):
+    last_units, written_units, written, sent = writer(
+        act_two, h0_ref, 2, out_parts, table, stage, order, tiles_ref, out_ref, out_hbm, left, 0
+    )
+
+    def steady(row, first=True):
         units = mixed(
-            written_units(0) + written_units(1) if row else [],
-            middle_units(row + 4) if middle else [],
+            written_units(0) + written_units(1) if row else [], middle_units(row + 4)
         )
-        units += mixed(last_units(row), inputs(row + 8) if first else [])
+        units += mixed(last_units(row) if row < early else [], inputs(row + 8) if first else [])
         pipelined(units)
         if row:
             written(row - 2)
             sent(row - 2).start()
+        if row + 4 >= early:
+            handing(row + 4 - early).start()
 
     pairs = rows // 2
     pipelined(inputs(0) + inputs(2))
     loop(0, 2, lambda row: pipelined(mixed(middle_units(row), inputs(row + 4))))
     loop(0, pairs - 2, steady)
-    loop(pairs - 2, pairs - 1, lambda row: steady(row, first=False))
-    loop(pairs - 1, pairs, lambda row: steady(row, middle=False, first=False))
-    pipelined(written_units(0) + written_units(1))
-    written(rows - 2)
-    sent(rows - 2).start()
-    weighted = jnp.sum(total[...] * table[5], keepdims=True)
+    for row in range(late + 2, 2 * late + 2, 2):
+        handing(row).start()
+    steady(rows - 4, first=False)
+    if early > rows - 4:
+        pipelined(written_units(0) + written_units(1))
+        written(early - 2)
+        sent(early - 2).start()
+
+    image = total[...] * table[5] + table[4] * table[5] * (count * rows)
+    halves = [image[:, :128], image[:, 128:]]
+    lane = lax.broadcasted_iota(jnp.int32, (channels, 128), 1)
+    for i in range(9):
+        down, later = i // 3, i % 3
+        read = sums[5 * later + down] + sums[5 * later + down + 1] + sums[5 * later + down + 2]
+        left_tap, middle_tap, right_tap = (
+            coefs[k, i * channels : (i + 1) * channels] for k in range(3)
+        )
+        own = left_tap + middle_tap + jnp.where(lane > 0, right_tap, 0.0)
+        halves[0] = halves[0] + read[:, :128] * own
+        own = middle_tap + right_tap + jnp.where(lane < 127, left_tap, 0.0)
+        halves[1] = halves[1] + read[:, 128:] * own
+    weighted = jnp.sum(halves[0] + halves[1], keepdims=True)
     sum_ref[...] = jnp.broadcast_to(weighted * flags[4:5, :128], sum_ref.shape)
-    for pair in range(pairs):
-        sent(2 * pair).wait()
+    for row in range(0, early, 2):
+        sent(row).wait()
+    for row in range(0, 2 * late + 2, 2):
+        handing(row).wait()
+
+
+def rest_kernel(
+    table, out_alone, out_both, out_rest, rest_hbm, begun, out_hbm,
+    rest, handed, out_ref, left, stage, order, tiles_ref,
+):
+    del begun
+    late, count, width = out_ref.shape[0], out_ref.shape[1], table.shape[2]
+    copies = []
+    for i, (row, end, frames) in enumerate(
+        ((0, late + 2, count + 2), (late + 2, 2 * late + 2, count))
+    ):
+        some = pl.ds(row, end - row), pl.ds(0, frames)
+        copies.append(pltpu.make_async_copy(rest_hbm.at[some], rest.at[some], handed.at[i]))
+    for copy in copies:
+        copy.start()
+    order_of_pixels(order, stage, width, count)
+    last_units, written_units, written, sent = writer(
+        rest, rest, late + 2, (out_alone, out_both, out_rest), table, stage, order, tiles_ref,
+        out_ref, out_hbm, left, out_hbm.shape[0] - late,
+    )
+    for copy in copies:
+        copy.wait()
+    for row in range(0, late + 2, 2):
+        units = written_units(0) + written_units(1) if row else []
+        pipelined(units + (last_units(row) if row < late else []))
+        if row:
+            written(row - 2)
+            sent(row - 2).start()
+    for row in range(0, late, 2):
+        sent(row).wait()
 
 
 def local(
@@ -344,7 +447,9 @@
     oldest = moved(own, POSITION, 2)
     padded = lax.optimization_barrier(jnp.pad(own, ((3, 3), (0, 0), (0, 0))))
     spans = (padded[3 : rows + 3], previous, oldest)
-    low = moved(jnp.concatenate([x[rows - 3 :] for x in spans], axis=0), "band", 1)
+    edge = jnp.concatenate([x[rows - 3 :] for x in spans], axis=0)
+    edge, mid_weight, out_weight = lax.optimization_barrier((edge, mid_weight, out_weight))
+    low = moved(edge, "band", 1)
     high = moved(jnp.concatenate([x[:3] for x in spans], axis=0), "band", -1)
 
     win = in_weight.transpose(2, 1, 0, 3).reshape(27, 3, channels).astype(F32)
@@ -360,45 +465,73 @@
     prepared = pl.pallas_call(
         prepared_kernel,
         in_specs=[vmem] * 4,
-        out_specs=[vmem] * 9,
+        out_specs=[vmem] * 10,
         out_shape=[
             jax.ShapeDtypeStruct((8, width), F32),
             jax.ShapeDtypeStruct((count * channels, 28 * SLOTS), BF16),
             jax.ShapeDtypeStruct((6, channels, width), F32),
+            jax.ShapeDtypeStruct((3, 3 * block, 128), F32),
         ] + [jax.ShapeDtypeStruct(shape, BF16) for shape in parts],
         compiler_params=pltpu.CompilerParams(vmem_limit_bytes=12 << 20),
         cost_estimate=pl.CostEstimate(flops=10**9, bytes_accessed=6 * 10**6, transcendentals=0),
     )(win, mid_weight.swapaxes(0, 1), out_weight.swapaxes(0, 1), cols)
-    features, weighted = pl.pallas_call(
+    late = rows // 6
+    early = rows - late
+    hbm = pl.BlockSpec(memory_space=pltpu.HBM)
+    out = jax.ShapeDtypeStruct((rows, count, width * channels), BF16)
+
+    kept = pltpu.VMEM((2 * late + 2, count + 2, channels, width), BF16)
+
+    def row_buffers(amount):
+        return [
+            pltpu.VMEM((amount, count, width * channels), BF16),
+            pltpu.SemaphoreType.DMA((amount // 2,)),
+        ]
+
+    ordering = [
+        pltpu.VMEM((2, count, 128, width), BF16),
+        pltpu.VMEM((width, width), BF16),
+        pltpu.VMEM((2, count, width * channels), F32),
+    ]
+    features, weighted, rest = pl.pallas_call(
         block_kernel,
-        in_specs=[vmem] * 14,
-        out_specs=[pl.BlockSpec(memory_space=pltpu.HBM), vmem],
+        in_specs=[vmem] * 15,
+        out_specs=[hbm, vmem, hbm],
         out_shape=[
-            jax.ShapeDtypeStruct((rows, count, width * channels), BF16),
+            out,
             jax.ShapeDtypeStruct((devices, 128), F32),
+            jax.ShapeDtypeStruct((HANDED,) + kept.shape[1:], BF16),
         ],
-        scratch_shapes=[
-            pltpu.VMEM((rows, count, width * channels), BF16),
-            pltpu.SemaphoreType.DMA((rows // 2,)),
+        scratch_shapes=[kept, pltpu.SemaphoreType.DMA((late + 1,))] + row_buffers(early) + [
             pltpu.VMEM((rows + 6, 2 * SLOTS, 3 * width), F32),
             pltpu.VMEM((9, rows + 6, 2 * SLOTS, width), F32),
             pltpu.VMEM((rows + 4, count + 4, channels, width), BF16),
-            pltpu.VMEM((rows + 2, count + 2, channels, width), BF16),
-            pltpu.VMEM((rows + 4, count, channels, width), BF16),
+            pltpu.VMEM((early + 2, count + 2, channels, width), BF16),
+            pltpu.VMEM((early + 2, count, channels, width), BF16),
             pltpu.VMEM((channels, width), F32),
-            pltpu.VMEM((2, count, 128, width), BF16),
-            pltpu.VMEM((width, width), BF16),
-            pltpu.VMEM((2, count, width * channels), F32),
-        ],
+            pltpu.VMEM((15, channels, width), F32),
+        ] + ordering,
         compiler_params=pltpu.CompilerParams(vmem_limit_bytes=32 << 20),
     )(*prepared, padded, previous, oldest, low, high)
+    weighted, clip_of = lax.optimization_barrier((weighted, segments))
+    gathered = lax.all_to_all(weighted, EVERY, 0, 0, tiled=True)
+    table, out_weights = prepared[2], prepared[-3:]
+    features = pl.pallas_call(
+        rest_kernel,
+        in_specs=[vmem] * 4 + [hbm] * 2,
+        out_specs=hbm,
+        out_shape=out,
+        scratch_shapes=[kept, pltpu.SemaphoreType.DMA((2,))] + row_buffers(late) + ordering,
+        input_output_aliases={5: 0},
+        compiler_params=pltpu.CompilerParams(vmem_limit_bytes=16 << 20),
+        cost_estimate=pl.CostEstimate(flops=5 * 10**9, bytes_accessed=10**7, transcendentals=0),
+    )(table, *out_weights, rest, features)
     features = features.transpose(1, 0, 2)
 
     clips = targets.shape[0]
-    gathered = lax.all_to_all(weighted, EVERY, 0, 0, tiled=True)
     part = jnp.sum(gathered[:, :clips], axis=0)
     labels = jnp.arange(clips, dtype=jnp.int32)
-    member = (segments[:, None] == labels[None, :]).astype(F32)
+    member = (clip_of[:, None] == labels[None, :]).astype(F32)
     cells = jnp.sum(member, axis=0) * (count * rows * lax.axis_size("band") * width)
     scores = part / cells + head_bias[0]
     loss = jnp.mean((scores - targets) ** 2)

time: 67.7 us -> 66.2 us (0.978)
  waiting for transfers between devices: 9.82 us -> 4.51 us
  Pallas kernels: 32.8 us -> 35.7 us
  local copies, waits for them, and re-layouts: 3.19 us -> 3.91 us
    all_to_all x1, waiting for transfers between devices: 6.35 us -> 2.51 us  [local(): gathered = lax.all_to_all(weighted, EVERY, 0, 0, tiled=True)]
    pallas_call x2 -> x3, Pallas kernels: 32.8 us -> 35.7 us  [the longest x1 29.9 us: local(): pl.pallas_call(block_kernel, in_specs=[vmem] * 15, out_specs=[hbm, vmem,...]
    ppermute x4, waiting for transfers between devices: 3.47 us -> 2 us  [moved(): return lax.ppermute(block, axis, route)]
    another operation x2, local copies, waits for them, and re-layouts: 0.03 us -> 0.78 us  [local(): jnp.stack([in_bias, gain_one, mid_bias, gain_two, out_bias, head_weight,...]
  transfers between devices with their start and end apart: 5 -> 5, of which waited for: 2 -> 2; matrix products, arithmetic and copies ran while one was open for 6% -> 7% of each run, Pallas kernels for 2% -> 9%
where the time goes in v5:
time: 66.2 us; the launch traced here: 65.7 us
  Pallas kernels  35.7 us (54%)
  starting transfers between devices  16.2 us (24%)
  waiting for transfers between devices  4.51 us (7%)
  local copies, waits for them, and re-layouts  3.91 us (6%)
  between operations  3.27 us (5%)
  other arithmetic  2.1 us (3%)
    pallas_call x1, Pallas kernels, local(): pl.pallas_call(block_kernel, in_specs=[vmem] * 15, out_specs=[hbm, vmem,...  29.9 us
    ppermute x4, starting transfers between devices, moved(): return lax.ppermute(block, axis, route)  13 us
    pallas_call x1, Pallas kernels, local(): pl.pallas_call(rest_kernel, in_specs=[vmem] * 4 + [hbm] * 2, out_specs=hb...  4.45 us
    all_to_all x1, starting transfers between devices, local(): gathered = lax.all_to_all(weighted, EVERY, 0, 0, tiled=True)  3.16 us
    all_to_all x1, waiting for transfers between devices, local(): gathered = lax.all_to_all(weighted, EVERY, 0, 0, tiled=True)  2.51 us
    ppermute x4, waiting for transfers between devices, moved(): return lax.ppermute(block, axis, route)  2 us
    transpose x1, local copies, waits for them, and re-layouts, local(): out_weight.swapaxes(0, 1)  1.38 us
    pallas_call x1, Pallas kernels, local(): pl.pallas_call(prepared_kernel, in_specs=[vmem] * 4, out_specs=[vmem] * 1...  1.35 us
  transfers between devices with their start and end apart: 5, of which 2 were waited for; matrix products, arithmetic and copies ran while one was open for 7% of the time, Pallas kernels for 9%

profile of v5, /device:TPU:0, one launch (start us, length us, event | category | flops | bytes accessed | tf_op | source)
XLA Modules:
  0.0 65.7 jit_solution(12577782825913063975)
XLA Ops:
  0.6 4.8 %collective-permute-start = (bf16[12,4,768]{2,1,0:T(4,128)(2,1)}, bf16[12,4,768]{2,1,0:T(4,128)(2,1)S(1)}, u32[]{:S(2)}, u32[]{:S(2)}) collective-permute-start(bf16[12,4,768]{2,1,0:T(4,128)(2,1)} %bitcast.24), channel_id=1, source_target_pairs={{0,4},{4,8},{8,12},{12,16},{16,20},{20,24},{24,28},{1,5},{5,9},{9,... | collective-permute-start | bytes 221192 | tf_op jit(solution)/shard_map/ppermute | solution.py:21
  5.5 3.4 %collective-permute-start.1 = (bf16[12,4,768]{2,1,0:T(4,128)(2,1)}, bf16[12,4,768]{2,1,0:T(4,128)(2,1)S(1)}, u32[]{:S(2)}, u32[]{:S(2)}) collective-permute-start(bf16[12,4,768]{2,1,0:T(4,128)(2,1)} %bitcast.25), channel_id=1, source_target_pairs={{0,8},{4,12},{8,16},{12,20},{16,24},{20,28},{1,9},{5,13},{9,17},{1... | collective-permute-start | bytes 221192 | tf_op jit(solution)/shard_map/ppermute | solution.py:21
  8.9 0.9 %pad.16.own_ref = bf16[18,4,768]{2,1,0:T(4,128)(2,1)S(1)} pad(bf16[12,4,768]{2,1,0:T(4,128)(2,1)} %bitcast.26, bf16[]{:T(256)} %constant.8.clone.1), padding=3_3x0_0x0_0 | pad | bytes 184322 | tf_op jit(solution)/shard_map/jit(_pad)/pad | solution.py:448
  9.9 0.8 %copy.24 = bf16[9,3,3,96]{3,2,1,0:T(4,128)(2,1)S(1)} copy(bf16[9,3,3,96]{3,1,0,2:T(4,128)(2,1)} %bitcast.28) | data formatting | bytes 31104 | tf_op jit(solution)/shard_map/convert_element_type | solution.py:455
  10.6 0.7 %convert_element_type.21 = f32[8]{0:T(128)S(1)} convert(s32[8]{0:T(128)} %param.14) | non-fusion elementwise | flops 8 | bytes 64 | tf_op jit(solution)/shard_map/convert_element_type | solution.py:457
  12.0 0.8 %stack.32.cols_ref = f32[8,96]{1,0:T(8,128)S(1)} concatenate(f32[1,96]{1,0:T(1,128)} %bitcast.29, f32[1,96]{1,0:T(1,128)} %bitcast.31, f32[1,96]{1,0:T(1,128)} %bitcast.32, f32[1,96]{1,0:T(1,128)} %bitcast.33, f32[1,96]{1,0:T(1,128)} %bitcast.34, f32[1,96]{1,0:T(1,128)} %bitcast.35, f32[1,96]{1,0:T(1,128)S(1)} %pad_bitcast_fusion, f32[1,96]{1,0:T(1,128)} %bitcast.30), dimensions={0} | concatenate | bytes 6144 | tf_op jit(solution)/shard_map/stack | solution.py:458
  12.8 0.0 collective-permute-done.previous_ref
  12.8 0.0 collective-permute-done.1.oldest_ref
  12.9 3.5 %collective-permute-start.2 = (bf16[9,4,768]{2,1,0:T(4,128)(2,1)S(1)}, bf16[9,4,768]{2,1,0:T(4,128)(2,1)S(1)}, u32[]{:S(2)}, u32[]{:S(2)}) collective-permute-start(bf16[9,4,768]{2,1,0:T(4,128)(2,1)S(1)} %pad_maximum_fusion), channel_id=1, source_target_pairs={{0,1},{1,2},{2,3},{4,5},{5,6},{6,7},{8,9},{9,10},{10,11},{12,13},{... | collective-permute-start | bytes 165896 | tf_op jit(solution)/shard_map/ppermute | solution.py:21
  16.4 1.3 %collective-permute-start.3 = (bf16[9,4,768]{2,1,0:T(4,128)(2,1)S(1)}, bf16[9,4,768]{2,1,0:T(4,128)(2,1)S(1)}, u32[]{:S(2)}, u32[]{:S(2)}) collective-permute-start(bf16[9,4,768]{2,1,0:T(4,128)(2,1)S(1)} %pad_maximum_fusion.1), channel_id=1, source_target_pairs={{1,0},{2,1},{3,2},{5,4},{6,5},{7,6},{9,8},{10,9},{11,10},{13,12},{... | collective-permute-start | bytes 165896 | tf_op jit(solution)/shard_map/ppermute | solution.py:21
  17.7 1.4 %copy_bitcast_fusion = (bf16[3,3,288,96]{3,2,1,0:T(8,128)(2,1)S(1)}, bf16[3,3,288,96]{3,2,1,0:T(8,128)(2,1)S(1)}) fusion(bf16[3,3,288,96]{3,2,1,0:T(8,128)(2,1)} %param.22, bf16[3,3,288,96]{3,2,1,0:T(8,128)(2,1)} %param.19), kind=kLoop, calls=%fused_computation | loop fusion | bytes 1990656 | tf_op jit(solution)/shard_map/transpose | solution.py:477
  19.1 1.4 %shard_map.148 = (f32[8,256]{1,0:T(8,128)S(1)}, bf16[384,224]{1,0:T(8,128)(2,1)S(1)}, f32[6,96,256]{2,1,0:T(8,128)S(1)}, f32[3,864,128]{2,1,0:T(8,128)S(1)}, bf1...) custom-call(f32[27,8,96]{2,1,0:T(8,128)S(1)} %pad_convert_fusion.win, ...), custom_call_target="tpu_custom_call" | custom-call | flops 1000000000 | bytes 6000000 | tf_op jit(solution)/shard_map/pallas_call | solution.py:465
  20.5 0.0 collective-permute-done.2.low_ref
  20.5 2.0 %collective-permute-done.3.high_ref = bf16[9,4,768]{2,1,0:T(4,128)(2,1)S(1)} collective-permute-done((bf16[9,4,768]{2,1,0:T(4,128)(2,1)S(1)}, bf16[9,4,768]{2,1,0:T(4,128)(2,1)S(1)}, u32[]{:S(2)}, u32[]{:S(2)}) %collective-permute-start.3) | collective-permute-done | bytes 55328 | tf_op jit(solution)/shard_map/ppermute | solution.py:21
  22.5 29.9 %shard_map.149 = (bf16[12,4,24576]{2,1,0:T(4,128)(2,1)}, f32[32,128]{1,0:T(8,128)}, bf16[160,6,96,256]{3,2,1,0:T(8,128)(2,1)}) custom-call(f32[8,256]{1,0:T(8,128)S(1)} %get-tuple-element.27.flags, bf16[384,224]{1,0:T(8,128)(2,1)S(1)} %get-tuple-element.28.win, f32[6,96,256]{2,1,0:T(8,128)S(1)} %get-tuple-element.23.table, ...), custom_call_target="tpu_custom_call" | custom-call | tf_op jit(solution)/shard_map/pallas_call | solution.py:496
  52.4 3.2 %all-to-all-start = ((f32[32,1,128]{2,1,0:T(1,128)}), f32[32,1,128]{2,1,0:T(1,128)S(1)}, u32[]{:S(2)}, u32[]{:S(2)}) async-start(f32[32,1,128]{2,1,0:T(1,128)} %bitcast.14), calls=%async_computation | async-start | bytes 32768 | tf_op jit(solution)/shard_map/all_to_all | solution.py:517
  55.6 0.0 copy-start.1
  55.6 0.0 copy-start
  55.6 4.4 %shard_map.150 = bf16[12,4,24576]{2,1,0:T(4,128)(2,1)} custom-call(f32[6,96,256]{2,1,0:T(8,128)S(1)} %get-tuple-element.23.table, bf16[288,256]{1,0:T(8,128)(2,1)S(1)} %get-tuple-element.24.out_alone, bf16[576,768]{1,0:T(8,128)(2,1)S(1)} %get-tuple-element.25.out_both, ...), custom_call_target="tpu_custom_call", output_to_operand_aliasing={{}: (5, {})} | custom-call | flops 5000000000 | bytes 10000000 | tf_op jit(solution)/shard_map/pallas_call | solution.py:519
  60.0 0.0 copy-done.1
  60.1 0.1 convert_reduce_fusion
  60.2 2.5 %all-to-all-done = f32[32,1,128]{2,1,0:T(1,128)S(1)} async-done(((f32[32,1,128]{2,1,0:T(1,128)}), f32[32,1,128]{2,1,0:T(1,128)S(1)}, u32[]{:S(2)}, u32[]{:S(2)}) %all-to-all-start) | async-done | bytes 16416 | tf_op jit(solution)/shard_map/all_to_all | solution.py:517
  62.7 0.0 copy-done
  62.7 1.2 %multiply_reduce_fusion = (f32[]{:T(128)}, f32[4]{0:T(128)}) fusion(f32[4]{0:T(128)S(1)} %copy-done, f32[]{:T(128)} %bitcast.21, f32[4]{0:T(128)S(1)} %slice_reduce_fusion, f32[4]{0:T(128)S(1)} %convert_reduce_fusion), kind=kLoop, calls=%fused_computation.8 | loop fusion | flops 23 | bytes 72 | tf_op jit(solution)/shard_map/reduce_sum | solution.py:537
  (8 shorter events, 0.2 us)
Async XLA Ops:
  0.6 12.1 %collective-permute-start = (bf16[12,4,768]{2,1,0:T(4,128)(2,1)}, bf16[12,4,768]{2,1,0:T(4,128)(2,1)S(1)}, u32[]{:S(2)}, u32[]{:S(2)}) collective-permute-start(bf16[12,4,768]{2,1,0:T(4,128)(2,1)} %bitcast.24), channel_id=1, source_target_pairs={{0,4},{4,8},{8,12},{12,16},{16,20},{20,24},{24,28},{1,5},{5,9},{9,... | collective-permute-start | bytes 221192 | tf_op jit(solution)/shard_map/ppermute | solution.py:21
  5.5 7.3 %collective-permute-start.1 = (bf16[12,4,768]{2,1,0:T(4,128)(2,1)}, bf16[12,4,768]{2,1,0:T(4,128)(2,1)S(1)}, u32[]{:S(2)}, u32[]{:S(2)}) collective-permute-start(bf16[12,4,768]{2,1,0:T(4,128)(2,1)} %bitcast.25), channel_id=1, source_target_pairs={{0,8},{4,12},{8,16},{12,20},{16,24},{20,28},{1,9},{5,13},{9,17},{1... | collective-permute-start | bytes 221192 | tf_op jit(solution)/shard_map/ppermute | solution.py:21
  12.9 7.6 %collective-permute-start.2 = (bf16[9,4,768]{2,1,0:T(4,128)(2,1)S(1)}, bf16[9,4,768]{2,1,0:T(4,128)(2,1)S(1)}, u32[]{:S(2)}, u32[]{:S(2)}) collective-permute-start(bf16[9,4,768]{2,1,0:T(4,128)(2,1)S(1)} %pad_maximum_fusion), channel_id=1, source_target_pairs={{0,1},{1,2},{2,3},{4,5},{5,6},{6,7},{8,9},{9,10},{10,11},{12,13},{... | collective-permute-start | bytes 165896 | tf_op jit(solution)/shard_map/ppermute | solution.py:21
  16.4 6.0 %collective-permute-start.3 = (bf16[9,4,768]{2,1,0:T(4,128)(2,1)S(1)}, bf16[9,4,768]{2,1,0:T(4,128)(2,1)S(1)}, u32[]{:S(2)}, u32[]{:S(2)}) collective-permute-start(bf16[9,4,768]{2,1,0:T(4,128)(2,1)S(1)} %pad_maximum_fusion.1), channel_id=1, source_target_pairs={{1,0},{2,1},{3,2},{5,4},{6,5},{7,6},{9,8},{10,9},{11,10},{13,12},{... | collective-permute-start | bytes 165896 | tf_op jit(solution)/shard_map/ppermute | solution.py:21
  52.4 10.3 %all-to-all-start = ((f32[32,1,128]{2,1,0:T(1,128)}), f32[32,1,128]{2,1,0:T(1,128)S(1)}, u32[]{:S(2)}, u32[]{:S(2)}) async-start(f32[32,1,128]{2,1,0:T(1,128)} %bitcast.14), calls=%async_computation | async-start | bytes 32768 | tf_op jit(solution)/shard_map/all_to_all | solution.py:517
  55.6 4.5 %copy-start.1 = (s32[8]{0:T(128)S(1)}, s32[8]{0:T(128)}, u32[]{:S(2)}) copy-start(s32[8]{0:T(128)} %param.14) | copy-start | bytes 100
  55.6 7.1 %copy-start = (f32[4]{0:T(128)S(1)}, f32[4]{0:T(128)}, u32[]{:S(2)}) copy-start(f32[4]{0:T(128)} %param.15) | copy-start | bytes 52
